TPU v7x, 256 devices: a whole 4x4x8 slice. The times are simulated.
256 devices in a mesh: dp: 64 (over z, y, core), mp: 4 (over x).
Axes of the slice: x: 4, y: 4, z: 8, core: 2. Of those that a mesh axis runs over, the one named last changes fastest.
Arguments:
- tokens: bfloat16 [128, 6656], P('dp', 'mp'), may hold values from -6 to 6
- grad_out: bfloat16 [128, 6656], P('dp', 'mp'), may hold values from -1.5 to 1.5
- gate_src: bfloat16 [10240, 6656], P(('dp', 'mp')), may hold values from -0.078125 to 0.078125
- up_src: bfloat16 [10240, 6656], P(('dp', 'mp')), may hold values from -0.078125 to 0.078125
- down_src: bfloat16 [10240, 6656], P(('dp', 'mp')), may hold values from -0.25 to 0.25
- unit_map: int32 [15360], P(('dp', 'mp')), may hold values from 0 to 10239, as said below
- copy_flag: int32 [15360], P(('dp', 'mp')), may hold values from 0 to 1, as said below
Outputs:
- layer_out: bfloat16 [128, 6656], P('dp', 'mp')
- grad_tokens: bfloat16 [128, 6656], P('dp', 'mp')
- grad_gate: bfloat16 [15360, 6656], P(('dp', 'mp'))
- grad_up: bfloat16 [15360, 6656], P(('dp', 'mp'))
- grad_down: bfloat16 [15360, 6656], P(('dp', 'mp'))
Inputs may be any that keep to these rules, and one draw needn't show every extreme that they name: `unit_map`: the widened unit j lies on the device of flat index j // 60 along dp+mp, and its source unit lies on a device with the same mp index. Every source unit is the source of one or two widened units. For every pair of devices, at most 3 widened units of the one have their source on the other; every device takes exactly 3 from some device and gives exactly 3 to some device. `copy_flag`: A source unit with one widened unit gives it flag 1; of a source's two widened units at least one has flag 1.
All inputs are finite; a program needn't handle non-finite values.
Results may differ from a plain program's by a relative error of at most 0.0049.
Values may be sent and summed in bfloat16 or wider, within the bound.
A program may use at most 128 MiB of HBM per device.

v0:
```python
import jax
import jax.numpy as jnp
from jax import lax
from jax.sharding import PartitionSpec as P


def layer_pass(inputs, cotangent, gate_rows, up_rows, down_rows):
    dims = (((1,), (1,)), ((), ()))
    pre_gate = lax.dot_general(inputs, gate_rows, dims, preferred_element_type=jnp.float32)
    pre_up = lax.dot_general(inputs, up_rows, dims, preferred_element_type=jnp.float32)
    sigma = jax.nn.sigmoid(pre_gate)
    active = pre_gate * sigma
    hidden = (active * pre_up).astype(jnp.bfloat16)
    out_part = jnp.dot(hidden, down_rows, preferred_element_type=jnp.float32)
    grad_hidden = lax.dot_general(cotangent, down_rows, dims, preferred_element_type=jnp.float32)
    grad_pre_gate = (grad_hidden * pre_up * (sigma + active * (1.0 - sigma))).astype(jnp.bfloat16)
    grad_pre_up = (grad_hidden * active).astype(jnp.bfloat16)
    input_part = jnp.dot(grad_pre_gate, gate_rows, preferred_element_type=jnp.float32)
    input_part = input_part + jnp.dot(grad_pre_up, up_rows, preferred_element_type=jnp.float32)
    tdims = (((0,), (0,)), ((), ()))
    gate_grad = lax.dot_general(
        grad_pre_gate, inputs, tdims, preferred_element_type=jnp.float32
    ).astype(jnp.bfloat16)
    up_grad = lax.dot_general(
        grad_pre_up, inputs, tdims, preferred_element_type=jnp.float32
    ).astype(jnp.bfloat16)
    down_grad = lax.dot_general(
        hidden, cotangent, tdims, preferred_element_type=jnp.float32
    ).astype(jnp.bfloat16)
    return (out_part, input_part, gate_grad, up_grad, down_grad)


def per_device(tokens, grad_out, gate_src, up_src, down_src, unit_map, copy_flag):
    n_dp = lax.axis_size("dp")
    n_mp = lax.axis_size("mp")
    src_dev = gate_src.shape[0]
    wide_dev = unit_map.shape[0]
    quant = (wide_dev + 3 * n_dp - 1) // (3 * n_dp)
    slots = 3 * quant
    my_mp = lax.axis_index("mp")
    my_flat = lax.axis_index("dp") * n_mp + my_mp
    unit_code = (unit_map * 2 + copy_flag).reshape(-1, 2)
    packed = unit_code[:, 0] + unit_code[:, 1] * 32768
    full_packed = lax.all_gather(packed, ("dp", "mp"), axis=0, tiled=True)
    lower_half = full_packed % 32768
    upper_half = full_packed // 32768
    full_code = jnp.stack([lower_half, upper_half], axis=1).reshape(-1)
    full_map = full_code // 2
    full_flag = full_code % 2
    share = jax.ops.segment_sum(
        full_flag.astype(jnp.float32), full_map, num_segments=src_dev * n_dp * n_mp
    )
    scale = copy_flag.astype(jnp.float32) / share[unit_map]
    owner_dp = unit_map // src_dev // n_mp
    unit_index = jnp.arange(wide_dev, dtype=jnp.int32)
    same_owner = (owner_dp[:, None] == owner_dp[None, :]) & (
        unit_index[:, None] > unit_index[None, :]
    )
    arrival = jnp.sum(same_owner.astype(jnp.int32), axis=1)
    recv_row = owner_dp * slots + arrival
    requests = lax.dynamic_index_in_dim(
        full_map.reshape(n_dp, n_mp, wide_dev), my_mp, 1, keepdims=False
    )
    owned = requests // src_dev == my_flat
    rank = jnp.cumsum(owned.astype(jnp.int32), axis=1) - 1
    slot_ids = jnp.arange(slots, dtype=jnp.int32)
    placed = owned[:, None, :] & (rank[:, None, :] == slot_ids[None, :, None])
    local = requests - my_flat * src_dev
    send_idx = jnp.sum(jnp.where(placed, local[:, None, :], 0), axis=2).reshape(-1)
    tok_feat, cot_feat = (
        lax.all_gather(tokens, "mp", axis=1, tiled=True),
        lax.all_gather(grad_out, "mp", axis=1, tiled=True),
    )
    inputs, cotangent = (
        lax.all_gather(tok_feat, "dp", axis=0, tiled=True),
        lax.all_gather(cot_feat, "dp", axis=0, tiled=True),
    )
    moved_gate, moved_up, moved_down = (
        lax.all_to_all(gate_src[send_idx], "dp", split_axis=0, concat_axis=0, tiled=True),
        lax.all_to_all(up_src[send_idx], "dp", split_axis=0, concat_axis=0, tiled=True),
        lax.all_to_all(down_src[send_idx], "dp", split_axis=0, concat_axis=0, tiled=True),
    )
    gate_wide = moved_gate[recv_row]
    up_wide = moved_up[recv_row]
    down_wide = (moved_down[recv_row].astype(jnp.float32) * scale[:, None]).astype(jnp.bfloat16)
    out_part, input_part, grad_gate, grad_up, grad_down = layer_pass(
        inputs, cotangent, gate_wide, up_wide, down_wide
    )
    out_cols, input_cols = (
        lax.psum_scatter(out_part, "mp", scatter_dimension=1, tiled=True),
        lax.psum_scatter(input_part, "mp", scatter_dimension=1, tiled=True),
    )
    out_sum, input_sum = (
        lax.psum_scatter(out_cols, "dp", scatter_dimension=0, tiled=True),
        lax.psum_scatter(input_cols, "dp", scatter_dimension=0, tiled=True),
    )
    return (
        out_sum.astype(jnp.bfloat16),
        input_sum.astype(jnp.bfloat16),
        grad_gate,
        grad_up,
        grad_down,
    )


def solution(mesh):
    in_specs = (
        P("dp", "mp"),
        P("dp", "mp"),
        P(("dp", "mp"), None),
        P(("dp", "mp"), None),
        P(("dp", "mp"), None),
        P(("dp", "mp")),
        P(("dp", "mp")),
    )
    out_specs = (
        P("dp", "mp"),
        P("dp", "mp"),
        P(("dp", "mp"), None),
        P(("dp", "mp"), None),
        P(("dp", "mp"), None),
    )
    return jax.shard_map(
        per_device, mesh=mesh, in_specs=in_specs, out_specs=out_specs, check_vma=False
    )
```

profile of v0, /device:TPU:1, one launch (start us, length us, event | category | flops | bytes accessed | tf_op | source)
XLA Modules:
  0.0 795.2 jit_solution(5214602645316661995)
XLA Ops:
  7.2 0.7 compare_select_fusion.4
  8.2 0.3 dynamic-update-slice
  8.5 81.4 %all-reduce = s32[7680]{0:T(1024)S(1)} all-reduce(s32[7680]{0:T(1024)S(1)} %dynamic-update-slice), channel_id=2, replica_groups=mesh['dp'=64,'mp'=4] {'dp','mp'}, use_global_device_ids=true, to_apply=%add | all-reduce | flops 7680 | bytes 61440 | tf_op jit(solution)/shard_map/all_gather | solution.py:44
  90.1 2.5 copy.21
  92.6 2.8 reshape.143
  95.5 0.4 fusion.4
  96.6 2.1 gather_fusion.4
  98.7 4.0 all_to_all.30
  102.7 6.8 all-to-all-start.2
  109.5 2.1 gather_fusion.2
  111.6 4.0 all_to_all.27
  115.6 72.0 %all-to-all-done.2 = bf16[64,3,6656]{2,1,0:T(4,128)(2,1)} async-done(((bf16[64,3,6656]{2,1,0:T(4,128)(2,1)}), bf16[64,3,6656]{2,1,0:T(4,128)(2,1)}, u32[]{:S(2)}, u32[]{:S(2)}) %all-to-all-start.2) | async-done | bytes 2555936 | tf_op jit(solution)/shard_map/all_to_all | solution.py:81
  187.6 6.8 all-to-all-start.1
  194.5 10.5 %all_gather.16 = bf16[2,6656]{1,0:T(2,128)(2,1)} all-gather(bf16[2,1664]{1,0:T(2,128)(2,1)S(1)} %copy-done.8), channel_id=1, replica_groups=mesh['dp'=64,'mp'=4] {'mp'}, dimensions={1}, use_global_device_ids=true | all-gather | bytes 33280 | tf_op jit(solution)/shard_map/all_gather | solution.py:71
  205.0 2.1 gather_fusion
  207.1 4.0 all_to_all.24
  211.1 64.2 %all-to-all-done.1 = bf16[64,3,6656]{2,1,0:T(4,128)(2,1)} async-done(((bf16[64,3,6656]{2,1,0:T(4,128)(2,1)}), bf16[64,3,6656]{2,1,0:T(4,128)(2,1)}, u32[]{:S(2)}, u32[]{:S(2)}) %all-to-all-start.1) | async-done | bytes 2555936 | tf_op jit(solution)/shard_map/all_to_all | solution.py:80
  275.4 7.0 all-to-all-start
  282.4 10.5 %all_gather.18 = bf16[2,6656]{1,0:T(2,128)(2,1)} all-gather(bf16[2,1664]{1,0:T(2,128)(2,1)S(1)} %copy-done.9), channel_id=1, replica_groups=mesh['dp'=64,'mp'=4] {'mp'}, dimensions={1}, use_global_device_ids=true | all-gather | bytes 33280 | tf_op jit(solution)/shard_map/all_gather | solution.py:72
  293.2 3.8 reshape.146
  297.0 5.3 reshape.145
  302.6 80.7 %scatter_custom_fusion = f32[10240]{0:T(1024)S(1)} fusion(s32[15360]{0:T(1024)S(1)} %bitcast.37, f32[15360]{0:T(1024)S(1)} %fusion.3, f32[]{:T(128)} %constant.106.clone.1), kind=kCustom, calls=%fused_computation.55 | custom fusion | flops 15360 | bytes 40964 | tf_op jit(solution)/shard_map/scatter-add | solution.py:50
  383.3 0.8 gather_fusion.6
  384.3 3.9 reshape.219
  388.3 4.7 reshape.221
  393.0 6.9 all_to_all.32
  399.9 4.7 gather_fusion.5
  404.7 6.9 all_to_all.29
  411.6 4.7 gather_fusion.3
  416.3 6.9 all_to_all.26
  423.3 3.8 gather_fusion.1
  427.1 2.0 convolution_bitcast_fusion.1
  429.1 0.7 convolution_bitcast_fusion.2
  429.8 0.7 multiply_convert_fusion.3
  430.6 0.6 fusion.14
  431.2 0.5 copy-done.7
  431.7 2.3 convolution_add_fusion
  434.2 1.1 copy-done.6
  435.2 2.4 fusion
  437.7 0.6 copy-done.11
  438.3 0.6 dynamic-slice
  439.6 2.7 convolution_convert_fusion
  442.3 1.3 convolution_convert_fusion.1
  443.6 1.3 convolution_convert_fusion.2
  444.9 33.9 %reduce-scatter.5.cloned.1.call-done = f32[128,1664]{1,0:T(8,128)} async-done(((f32[128,6656]{1,0:T(8,128)}), f32[128,1664]{1,0:T(8,128)}) %reduce-scatter.5.cloned.1.call-update) | async-done | bytes 851984 | tf_op jit(solution)/shard_map/reduce_scatter | solution.py:91
  478.8 45.1 %reduce-scatter.3.cloned.1.call-done = f32[128,1664]{1,0:T(8,128)} async-done(((f32[128,6656]{1,0:T(8,128)}), f32[128,1664]{1,0:T(8,128)}) %reduce-scatter.3.cloned.1.call-update) | async-done | bytes 851984 | tf_op jit(solution)/shard_map/reduce_scatter | solution.py:90
  523.9 264.2 %all-reduce.5 = (bf16[128,1664]{1,0:T(8,128)(2,1)S(1)}, bf16[128,1664]{1,0:T(8,128)(2,1)S(1)}) all-reduce(f32[128,1664]{1,0:T(8,128)} %reduce-scatter.3.cloned.1.call-done, f32[128,1664]{1,0:T(8,128)} %reduce-scatter.5.cloned.1.call-done), channel_id=4, replica_groups=mesh['dp'=64,'mp'=4] {'dp'}, use_global_device_ids=true, to_apply=%region_5.6.clone | all-reduce | flops 425984 | bytes 2555904
  788.1 0.6 dynamic-slice_convert_fusion
  (57 shorter events, 2.1 us)
Async XLA Ops:
  7.2 89.4 %copy-start = (bf16[40,6656]{1,0:T(8,128)(2,1)S(1)}, bf16[40,6656]{1,0:T(8,128)(2,1)}, u32[]{:S(2)}) copy-start(bf16[40,6656]{1,0:T(8,128)(2,1)} %param.11) | copy-start | bytes 1597444
  102.7 6.8 copy-start.2
  102.7 84.9 %all-to-all-start.2 = ((bf16[64,3,6656]{2,1,0:T(4,128)(2,1)}), bf16[64,3,6656]{2,1,0:T(4,128)(2,1)}, u32[]{:S(2)}, u32[]{:S(2)}) async-start(bf16[64,3,6656]{2,1,0:T(4,128)(2,1)} %all_to_all.30), calls=%async_computation.2 | async-start | bytes 6815744 | tf_op jit(solution)/shard_map/all_to_all | solution.py:81
  115.6 78.8 %copy-start.8 = (bf16[2,1664]{1,0:T(2,128)(2,1)S(1)}, bf16[2,1664]{1,0:T(2,128)(2,1)}, u32[]{:S(2)}) copy-start(bf16[2,1664]{1,0:T(2,128)(2,1)} %param.7) | copy-start | bytes 19972
  115.6 89.4 %copy-start.3 = (bf16[40,6656]{1,0:T(8,128)(2,1)S(1)}, bf16[40,6656]{1,0:T(8,128)(2,1)}, u32[]{:S(2)}) copy-start(bf16[40,6656]{1,0:T(8,128)(2,1)} %param.9) | copy-start | bytes 1597444
  187.6 87.8 %all-to-all-start.1 = ((bf16[64,3,6656]{2,1,0:T(4,128)(2,1)}), bf16[64,3,6656]{2,1,0:T(4,128)(2,1)}, u32[]{:S(2)}, u32[]{:S(2)}) async-start(bf16[64,3,6656]{2,1,0:T(4,128)(2,1)} %all_to_all.27), calls=%async_computation.1 | async-start | bytes 6815744 | tf_op jit(solution)/shard_map/all_to_all | solution.py:80
  194.4 189.9 %all-gather.6.cloned.1.call-start = ((), (), s32[]{:S(2)}) async-start(), calls=%async_computation.7 | async-start | bytes 1730560 | tf_op jit(solution)/shard_map/all_gather | solution.py:75
  211.1 71.3 %copy-start.9 = (bf16[2,1664]{1,0:T(2,128)(2,1)S(1)}, bf16[2,1664]{1,0:T(2,128)(2,1)}, u32[]{:S(2)}) copy-start(bf16[2,1664]{1,0:T(2,128)(2,1)} %param.8) | copy-start | bytes 19972
  275.4 141.0 %all-to-all-start = ((bf16[64,3,6656]{2,1,0:T(4,128)(2,1)}), bf16[64,3,6656]{2,1,0:T(4,128)(2,1)}, u32[]{:S(2)}, u32[]{:S(2)}) async-start(bf16[64,3,6656]{2,1,0:T(4,128)(2,1)} %all_to_all.24), calls=%async_computation | async-start | bytes 6815744 | tf_op jit(solution)/shard_map/all_to_all | solution.py:79
  282.4 105.9 %all-gather.8.cloned.1.call-start = ((), (), s32[]{:S(2)}) async-start(), calls=%async_computation.8 | async-start | bytes 1730560 | tf_op jit(solution)/shard_map/all_gather | solution.py:76
  293.0 185.8 %reduce-scatter.5.cloned.1.call-start = ((), (), s32[]{:S(2)}) async-start(), calls=%async_computation.6 | async-start | bytes 4259840 | tf_op jit(solution)/shard_map/reduce_scatter | solution.py:91
  297.0 87.3 %copy-start.10 = (s32[60]{0:T(128)S(1)}, s32[60]{0:T(128)}, u32[]{:S(2)}) copy-start(s32[60]{0:T(128)} %param.13) | copy-start | bytes 724
  427.1 2.7 copy-start.4
  427.1 2.7 copy-start.5
  430.6 1.2 copy-start.7
  434.1 1.2 copy-start.6
  434.1 89.8 %reduce-scatter.3.cloned.1.call-start = ((), (), s32[]{:S(2)}) async-start(), calls=%async_computation.5 | async-start | bytes 4259840 | tf_op jit(solution)/shard_map/reduce_scatter | solution.py:90
  437.7 0.7 copy-start.11
  442.3 346.4 %copy-start.1 = (bf16[40,6656]{1,0:T(8,128)(2,1)S(1)}, bf16[40,6656]{1,0:T(8,128)(2,1)}, u32[]{:S(2)}) copy-start(bf16[40,6656]{1,0:T(8,128)(2,1)} %param.11) | copy-start | bytes 1597444
Sparse Core Ops, SparseCore 0:
  205.1 85.4 all-gather.5
  293.3 84.3 all-gather.7
  434.2 44.5 reduce-scatter.4
  481.2 42.6 reduce-scatter.2
where the time goes:
time: 800 us; the launch traced here: 795 us
  blocking collectives  367 us (46%)
  waiting for transfers between devices  215 us (27%)
  other arithmetic  83.1 us (10%)
  local copies, waits for them, and re-layouts  80.3 us (10%)
  starting transfers between devices  20.9 us (3%)
  between operations  14.9 us (2%)
  matrix products  14.1 us (2%)
    unnamed x1, blocking collectives  264 us
    all_gather x1, blocking collectives, per_device(): full_packed = lax.all_gather(packed, ('dp', 'mp'), axis=0, tiled=True)  81.4 us
    scatter-add x1, other arithmetic, per_device(): jax.ops.segment_sum(full_flag.astype(jnp.float32), full_map, num_segments...  80.7 us
    all_to_all x1, waiting for transfers between devices, per_device(): lax.all_to_all(down_src[send_idx], 'dp', split_axis=0, concat_axis=0, til...  72 us
    all_to_all x1, waiting for transfers between devices, per_device(): lax.all_to_all(up_src[send_idx], 'dp', split_axis=0, concat_axis=0, tiled...  64.2 us
    reduce_scatter x1, waiting for transfers between devices, per_device(): lax.psum_scatter(out_part, 'mp', scatter_dimension=1, tiled=True)  45.1 us
    reduce_scatter x1, waiting for transfers between devices, per_device(): lax.psum_scatter(input_part, 'mp', scatter_dimension=1, tiled=True)  33.9 us
  transfers between devices with their start and end apart: 7, of which 4 were waited for; matrix products, arithmetic and copies ran while one was open for 15% of the time, Pallas kernels for 0%

commit v1 on v0

v1 whole, which is shorter than its diff:
```python
import functools

import jax
import jax.numpy as jnp
from jax import lax
from jax.experimental import pallas as pl
from jax.experimental.pallas import tpu as pltpu
from jax.sharding import PartitionSpec as P

MESH = pl.DeviceIdType.MESH
BF = jnp.bfloat16
F32 = jnp.float32
I32 = jnp.int32

CORES = 2
CHIPS_Y = 4
SLOTS = 3
LANES = 128
ROWS = 16


def _mod(v, n):
    return lax.rem(v + n, n)


class Geometry:
    def __init__(self, n_dp, n_mp, tokens_dev, cols, src, wide):
        self.Y = CHIPS_Y
        self.YC = CHIPS_Y * CORES
        self.Z = n_dp // self.YC
        self.X = n_mp
        self.dp = n_dp
        self.t = tokens_dev
        self.T = n_dp * tokens_dev
        self.G = self.YC * tokens_dev
        self.cols = cols
        tiles = cols // LANES
        self.a = (tiles // 2) * LANES
        self.b = cols - self.a
        self.D = cols * n_mp
        self.src = src
        self.R = -(-src // 16) * 16
        self.wide = wide
        self.W8 = -(-wide // 8) * 8
        self.long = self.Z // 2
        self.short = self.Z - 1 - self.long


def kernel(g, *refs):
    (tok, gro, gate_h, up_h, down_h, umap, flag, o_out, o_in, gg_h, gu_h, gd_h) = refs[:12]
    (
        s1_src, s1_rcv, asm, codes, own_code,
        buf_a, buf_b,
        w_gate, w_up, w_down, ws,
        lf, lb, lt,
        ss, sel, msg, r1, r2,
        sib_a, sib_b, rcv_a, rcv_b, pa, pb,
        ring_sl, ring_rl, ring_ss, ring_rs, ax_s, ax_r,
        bx_s, bx_r, bz_s, bz_r, sum_b,
        fin_s, fin_r,
        g_gate, g_up, g_down,
        w_sem, o_sem,
        s1_ss, s1_rs, cz_ss, cz_rs, ga_xs, ga_xr, ga_zs, ga_zr, gb_zs, gb_zr, gb_xs, gb_xr,
        sa_s, sa_r, sb_s, sb_r,
        m1_s, m1_r, m2_s, m2_r,
        ra_s, ra_r, rb_s, rb_r,
        rl_s, rl_r, rs_s, rs_r, axx_s, axx_r, bxx_s, bxx_r, bzz_s, bzz_r, f_s, f_r,
    ) = refs[12:]
    X, Y, Z, YC = g.X, g.Y, g.Z, g.YC
    dp = lax.axis_index("dp")
    x = lax.axis_index("mp")
    z = lax.div(dp, YC)
    yc = lax.rem(dp, YC)
    y = lax.div(yc, CORES)
    c = lax.rem(yc, CORES)
    other = 1 - c
    step = 1 - 2 * c

    def at_z(zz):
        return (zz * YC + yc, x)

    def at_x(xx):
        return (dp, xx)

    def at_yc(k):
        return (z * YC + k, x)

    sibling = at_yc(y * CORES + other)
    yc_peers = []
    for dy in range(Y):
        for dc in range(CORES):
            if dy or dc:
                py = _mod(y + dy, Y)
                pc = _mod(c + dc, CORES)
                qy = _mod(y - dy, Y)
                yc_peers.append((dy * CORES + dc, py * CORES + pc, pc, qy * CORES + pc))

    sent = []

    def copy(src, dst, s_sem, r_sem, device):
        return pltpu.make_async_remote_copy(
            src_ref=src, dst_ref=dst, send_sem=s_sem, recv_sem=r_sem,
            device_id=device, device_id_type=MESH,
        )

    def send(src, dst, s_sem, r_sem, device):
        op = copy(src, dst, s_sem, r_sem, device)
        op.start()
        sent.append(op)

    def arrive(dst, s_sem, r_sem, device):
        copy(dst, dst, s_sem, r_sem, device).wait_recv()

    bar = pltpu.get_barrier_semaphore()
    for k in range(1, X):
        pl.semaphore_signal(bar, inc=1, device_id=at_x(_mod(x + k, X)), device_id_type=MESH)
    for k in range(1, Z):
        pl.semaphore_signal(bar, inc=1, device_id=at_z(_mod(z + k, Z)), device_id_type=MESH)
    for _, peer, _, _ in yc_peers:
        pl.semaphore_signal(bar, inc=1, device_id=at_yc(peer), device_id_type=MESH)

    loads = [
        pltpu.make_async_copy(h, v, w_sem.at[i])
        for i, (h, v) in enumerate(((gate_h, w_gate), (up_h, w_up), (down_h, w_down)))
    ]
    for op in loads:
        op.start()

    code = umap[...] * 2 + flag[...]
    own_code[...] = jnp.full(own_code.shape, -1, I32)
    own_code[:, 0:g.wide] = code
    code_row = own_code[...]
    s1_src[0, :, 0:g.cols] = tok[...].astype(F32)
    s1_src[1, :, 0:g.cols] = gro[...].astype(F32)
    for k in range(2):
        s1_src[k, :, g.cols:g.cols + LANES] = jnp.broadcast_to(code_row.astype(F32), (g.t, LANES))
    s1_rcv[yc] = s1_src[c]

    pl.semaphore_wait(bar, (X - 1) + (Z - 1) + len(yc_peers))

    for i, peer, pc, _ in yc_peers:
        send(s1_src.at[pc], s1_rcv.at[yc], s1_ss.at[i], s1_rs.at[i], at_yc(peer))
    for i, _, _, origin in yc_peers:
        arrive(s1_rcv.at[origin], s1_ss.at[i], s1_rs.at[i], sibling)
    for k in range(YC):
        asm[k * g.t:(k + 1) * g.t, :] = s1_rcv[k, :, 0:g.cols]
        codes[z, k:k + 1, :] = s1_rcv[k, 0:1, g.cols:g.cols + LANES]
    block = asm[...].astype(BF)
    buf_a[c, z, x] = block[:, 0:g.a]
    buf_b[c, x, z] = block[:, g.a:g.cols]

    for k in range(1, X):
        send(buf_a.at[c, z, x], buf_a.at[c, z, x], ga_xs.at[k - 1], ga_xr.at[k - 1], at_x(_mod(x + k, X)))
    for k in range(1, Z):
        send(buf_b.at[c, x, z], buf_b.at[c, x, z], gb_zs.at[k - 1], gb_zr.at[k - 1], at_z(_mod(z + k, Z)))
    for k in range(1, Z):
        send(codes.at[z], codes.at[z], cz_ss.at[k - 1], cz_rs.at[k - 1], at_z(_mod(z + k, Z)))

    for op in loads:
        op.wait()
    ws[0, g.R:2 * g.R, :] = jnp.zeros((g.R, g.D), BF)
    if g.R > g.src:
        pad = jnp.zeros((16, g.D), BF)
        ws[0, g.R - 16:g.R, :] = pad
        ws[1, g.R - 16:g.R, :] = pad
        ws[1, 2 * g.R - 16:2 * g.R, :] = pad
    ws[0, 0:g.src, :] = w_down[...]
    ws[1, 0:g.src, :] = w_gate[...]
    ws[1, g.R:g.R + g.src, :] = w_up[...]

    for k in range(1, X):
        arrive(buf_a.at[c, z, _mod(x - k, X)], ga_xs.at[k - 1], ga_xr.at[k - 1], sibling)

    def ring_gather(hop):
        if hop < g.long:
            b = _mod(z - hop * step, Z)
            send(buf_a.at[c, b], buf_a.at[c, b], ga_zs.at[hop], ga_zr.at[hop], at_z(_mod(z + step, Z)))
        if hop < g.short:
            b = _mod(z + hop * step, Z)
            i = g.long + hop
            send(buf_a.at[c, b], buf_a.at[c, b], ga_zs.at[i], ga_zr.at[i], at_z(_mod(z - step, Z)))

    def share_a(b, i):
        send(buf_a.at[c, b], buf_a.at[c, b], sa_s.at[i], sa_r.at[i], sibling)

    ring_gather(0)
    share_a(z, 0)
    for k in range(1, Z):
        arrive(buf_b.at[c, x, _mod(z - k, Z)], gb_zs.at[k - 1], gb_zr.at[k - 1], sibling)
    for k in range(1, X):
        send(buf_b.at[c, x], buf_b.at[c, x], gb_xs.at[k - 1], gb_xr.at[k - 1], at_x(_mod(x + k, X)))
    send(buf_b.at[c, x], buf_b.at[c, x], sb_s.at[0], sb_r.at[0], sibling)
    for hop in range(1, g.long + 1):
        b = _mod(z - hop * step, Z)
        arrive(buf_a.at[c, b], ga_zs.at[hop - 1], ga_zr.at[hop - 1], sibling)
        b2 = _mod(z + hop * step, Z)
        if hop <= g.short:
            arrive(buf_a.at[c, b2], ga_zs.at[g.long + hop - 1], ga_zr.at[g.long + hop - 1], sibling)
        ring_gather(hop)
        share_a(b, hop)
        if hop <= g.short:
            share_a(b2, g.long + hop)

        if hop == 1:
            for k in range(1, Z):
                arrive(codes.at[_mod(z - k, Z)], cz_ss.at[k - 1], cz_rs.at[k - 1], sibling)
            routing(g, codes, ss, sel, dp * X + x)
    for k in range(1, X):
        xx = _mod(x - k, X)
        arrive(buf_b.at[c, xx], gb_xs.at[k - 1], gb_xr.at[k - 1], sibling)
        send(buf_b.at[c, xx], buf_b.at[c, xx], sb_s.at[k], sb_r.at[k], sibling)

    for k in range(g.long + 1):
        arrive(buf_a.at[other, _mod(z + k * step, Z)], sa_s.at[k], sa_r.at[k], sibling)
    for k in range(1, g.short + 1):
        arrive(buf_a.at[other, _mod(z - k * step, Z)], sa_s.at[g.long + k], sa_r.at[g.long + k], sibling)
    for k in range(X):
        arrive(buf_b.at[other, _mod(x - k, X)], sb_s.at[k], sb_r.at[k], sibling)

    nt = (((1,), (1,)), ((), ()))

    def rows_a(array, xx):
        return buf_a[array, :, xx].reshape(g.T, g.a)

    def rows_b(array, xx):
        return buf_b[array, xx].reshape(g.T, g.b)

    pre = jnp.zeros((2 * g.R, g.T), F32)
    gh = jnp.zeros((g.R, g.T), F32)
    for xx in range(X):
        lo, mid, hi = xx * g.cols, xx * g.cols + g.a, (xx + 1) * g.cols
        pre += lax.dot_general(ws[1, :, lo:mid], rows_a(0, xx), nt, preferred_element_type=F32)
        pre += lax.dot_general(ws[1, :, mid:hi], rows_b(0, xx), nt, preferred_element_type=F32)
        gh += lax.dot_general(ws[0, 0:g.R, lo:mid], rows_a(1, xx), nt, preferred_element_type=F32)
        gh += lax.dot_general(ws[0, 0:g.R, mid:hi], rows_b(1, xx), nt, preferred_element_type=F32)
    pre_gate = pre[0:g.src]
    pre_up = pre[g.R:g.R + g.src]
    gh = gh[0:g.src]
    sigma = jax.nn.sigmoid(pre_gate)
    active = pre_gate * sigma
    lf[...] = jnp.zeros(lf.shape, F32)
    lf[0, 0:g.src, :] = active * pre_up
    lf[1, 0:g.src, :] = gh * pre_up * (sigma + active * (1.0 - sigma))
    lf[1, g.R:g.R + g.src, :] = gh * active
    for k in range(2):
        lb[k * LANES:(k + 1) * LANES, :] = lf[k].astype(BF)
        lt[k] = lf[k].T.astype(BF)

    def partial(array, lo, hi):
        return jnp.dot(lt[array][:, 0:2 * g.R], ws[array, :, lo:hi], preferred_element_type=F32)

    for xx in range(X):
        lo = xx * g.cols
        sib_a[xx] = partial(other, lo, lo + g.a).astype(BF).reshape(Z, g.G, g.a)
        send(sib_a.at[xx], rcv_a.at[xx], ra_s.at[xx], ra_r.at[xx], sibling)
    for xx in range(X):
        lo = xx * g.cols
        sib_b[xx] = partial(other, lo + g.a, lo + g.cols).astype(BF).reshape(Z, g.G, g.b)
        send(sib_b.at[xx], rcv_b.at[xx], rb_s.at[xx], rb_r.at[xx], sibling)
    for xx in range(X):
        lo = xx * g.cols
        pa[xx] = partial(c, lo, lo + g.a).reshape(Z, g.G, g.a)
    for xx in range(X):
        arrive(rcv_a.at[xx], ra_s.at[xx], ra_r.at[xx], sibling)

    def own_a(b):
        return pa[:, b] + rcv_a[:, b].astype(F32)

    def ring_reduce(hop):
        if hop < g.long:
            v = own_a(_mod(z + (g.long - hop) * step, Z))
            if hop:
                arrive(ring_rl.at[hop - 1], rl_s.at[hop - 1], rl_r.at[hop - 1], sibling)
                v = v + ring_rl[hop - 1].astype(F32)
            ring_sl[hop] = v.astype(BF)
            send(ring_sl.at[hop], ring_rl.at[hop], rl_s.at[hop], rl_r.at[hop], at_z(_mod(z + step, Z)))
        if hop < g.short:
            v = own_a(_mod(z - (g.short - hop) * step, Z))
            if hop:
                arrive(ring_rs.at[hop - 1], rs_s.at[hop - 1], rs_r.at[hop - 1], sibling)
                v = v + ring_rs[hop - 1].astype(F32)
            ring_ss[hop] = v.astype(BF)
            send(ring_ss.at[hop], ring_rs.at[hop], rs_s.at[hop], rs_r.at[hop], at_z(_mod(z - step, Z)))

    ring_reduce(0)

    picked = jnp.dot(sel[...], lb[...], preferred_element_type=F32).astype(BF)
    msg[...] = picked.reshape(Z, YC, ROWS, g.T)
    r1[z] = msg[z]
    for k in range(1, Z):
        zz = _mod(z + k, Z)
        send(msg.at[zz], r1.at[z], m1_s.at[k - 1], m1_r.at[k - 1], at_z(zz))

    for k in range(X):
        xx = _mod(x + k + 1, X)
        lo = pl.multiple_of(xx * g.cols + g.a, LANES)
        v = jnp.dot(lt[c][:, 0:2 * g.R], ws[c, :, pl.ds(lo, g.b)], preferred_element_type=F32)
        arrive(rcv_b.at[xx], rb_s.at[xx], rb_r.at[xx], sibling)
        v = v.reshape(Z, g.G, g.b) + rcv_b[xx].astype(F32)
        if k < X - 1:
            bx_s[k] = v.astype(BF)
            send(bx_s.at[k], bx_r.at[k], bxx_s.at[k], bxx_r.at[k], at_x(xx))
        else:
            pb[...] = v

    for hop in range(1, g.long):
        ring_reduce(hop)

    for k in range(1, Z):
        arrive(r1.at[_mod(z - k, Z)], m1_s.at[k - 1], m1_r.at[k - 1], sibling)
    r2[yc] = r1[:, yc]
    for i, peer, _, _ in yc_peers:
        send(r1.at[:, peer], r2.at[yc], m2_s.at[i], m2_r.at[i], at_yc(peer))

    for k in range(X - 1):
        arrive(bx_r.at[k], bxx_s.at[k], bxx_r.at[k], sibling)
    total_b = pb[...]
    for k in range(X - 1):
        total_b = total_b + bx_r[k].astype(F32)
    sum_b[...] = total_b
    bz_s[...] = total_b.astype(BF)
    for k in range(1, Z):
        zz = _mod(z + k, Z)
        send(bz_s.at[zz], bz_r.at[k - 1], bzz_s.at[k - 1], bzz_r.at[k - 1], at_z(zz))

    v = own_a(z)
    if g.long:
        arrive(ring_rl.at[g.long - 1], rl_s.at[g.long - 1], rl_r.at[g.long - 1], sibling)
        v = v + ring_rl[g.long - 1].astype(F32)
    if g.short:
        arrive(ring_rs.at[g.short - 1], rs_s.at[g.short - 1], rs_r.at[g.short - 1], sibling)
        v = v + ring_rs[g.short - 1].astype(F32)
    pa[:, z] = v
    ax_s[...] = v.astype(BF)
    for k in range(1, X):
        xx = _mod(x + k, X)
        send(ax_s.at[xx], ax_r.at[k - 1], axx_s.at[k - 1], axx_r.at[k - 1], at_x(xx))

    for i, _, _, origin in yc_peers:
        arrive(r2.at[origin], m2_s.at[i], m2_r.at[i], sibling)
    wide = widened(g, own_code[...], r2)
    g_rows = jnp.concatenate([wide[1], wide[2]], axis=0)
    for xx in range(X):
        for lo, width, rows in (
            (xx * g.cols, g.a, rows_a),
            (xx * g.cols + g.a, g.b, rows_b),
        ):
            both = jnp.dot(g_rows, rows(0, xx), preferred_element_type=F32).astype(BF)
            g_gate[:, lo:lo + width] = both[0:g.wide]
            g_up[:, lo:lo + width] = both[g.W8:g.W8 + g.wide]
            down = jnp.dot(wide[0], rows(1, xx), preferred_element_type=F32).astype(BF)
            g_down[:, lo:lo + width] = down[0:g.wide]
    stores = [
        pltpu.make_async_copy(v, h, o_sem.at[i])
        for i, (v, h) in enumerate(((g_gate, gg_h), (g_up, gu_h), (g_down, gd_h)))
    ]
    for op in stores:
        op.start()

    va = pa[x, z]
    for k in range(1, X):
        arrive(ax_r.at[k - 1], axx_s.at[k - 1], axx_r.at[k - 1], sibling)
        va = va + ax_r[k - 1].astype(F32)
    vb = sum_b[z]
    for k in range(1, Z):
        arrive(bz_r.at[k - 1], bzz_s.at[k - 1], bzz_r.at[k - 1], sibling)
        vb = vb + bz_r[k - 1].astype(F32)
    for k in range(YC):
        fin_s[k, :, 0:g.a] = va[k * g.t:(k + 1) * g.t]
        fin_s[k, :, g.a:g.cols] = vb[k * g.t:(k + 1) * g.t]
    fin_r[yc] = fin_s[yc]
    for i, peer, _, _ in yc_peers:
        send(fin_s.at[peer], fin_r.at[yc], f_s.at[i], f_r.at[i], at_yc(peer))
    for i, _, _, origin in yc_peers:
        arrive(fin_r.at[origin], f_s.at[i], f_r.at[i], sibling)
    for k, out in enumerate((o_out, o_in)):
        total = fin_r[k]
        for yy in range(1, Y):
            total = total + fin_r[yy * CORES + k]
        out[...] = total.astype(BF)

    for op in stores:
        op.wait()
    for op in sent:
        op.wait_send()


def routing(g, codes, ss, sel, flat):
    n, Z, YC = g.dp, g.Z, g.YC
    c = codes[...].reshape(n, LANES).astype(I32)
    local = (c >> 1) - flat * g.src
    owned = (local >= 0) & (local < g.src)
    loc = local.astype(F32)
    flg = (c & 1).astype(F32)
    ownf = jnp.where(owned, 1.0, 0.0)
    before = lax.broadcasted_iota(I32, (LANES, LANES), 0) < lax.broadcasted_iota(I32, (LANES, LANES), 1)
    rank = jnp.dot(ownf.astype(BF), jnp.where(before, 1.0, 0.0).astype(BF), preferred_element_type=F32)
    lane = lax.broadcasted_iota(I32, (n, LANES), 1).astype(F32)
    wide_lane = lax.broadcasted_iota(I32, (n, 2 * LANES), 1).astype(F32)
    picks = []
    share = jnp.zeros((1, LANES), F32)
    for k in range(SLOTS):
        chosen = jnp.where(rank == float(k), ownf, 0.0)
        idx = jnp.sum(chosen * loc, axis=1, keepdims=True)
        has = jnp.sum(chosen, axis=1, keepdims=True)
        fl = jnp.sum(chosen * flg, axis=1, keepdims=True)
        one = jnp.where(lane == idx, has, 0.0)
        share = share + jnp.sum(one * fl, axis=0, keepdims=True)
        picks.append((idx, has, fl, one))
    for k, (idx, has, fl, one) in enumerate(picks):
        total = jnp.sum(one * share, axis=1, keepdims=True)
        scale = jnp.where(has > 0.0, fl / jnp.where(has > 0.0, total, 1.0), 0.0)
        for kind, (offset, factor) in enumerate(
            ((0.0, has), (float(LANES), scale), (float(LANES + g.R), scale))
        ):
            q = k * 3 + kind
            ss[q * n:(q + 1) * n, :] = jnp.where(wide_lane == idx + offset, factor, 0.0).astype(BF)
    q = 3 * SLOTS
    row = lax.broadcasted_iota(I32, (n * ROWS, q * n), 0)
    col = lax.broadcasted_iota(I32, (n * ROWS, q * n), 1)
    spread = jnp.where(col == (row & (ROWS - 1)) * n + (row >> 4), 1.0, 0.0).astype(BF)
    sel[...] = jnp.dot(spread, ss[...], preferred_element_type=F32).astype(BF)


def widened(g, code_row, r2):
    src = (code_row >> 1).astype(F32)
    owner = jnp.floor((src + 0.5) * (1.0 / (g.src * g.X)))
    zz = jnp.floor((owner + 0.5) * (1.0 / g.YC))
    first = ((owner - zz * g.YC) * g.Z + zz) * ROWS
    sub = lax.broadcasted_iota(I32, (LANES, LANES), 0)
    lane = lax.broadcasted_iota(I32, (LANES, LANES), 1)
    owners = jnp.broadcast_to(owner, (LANES, LANES))
    own_col = jnp.sum(jnp.where(sub == lane, owners, 0.0), axis=1, keepdims=True)
    first_col = jnp.sum(
        jnp.where(sub == lane, jnp.broadcast_to(first, (LANES, LANES)), 0.0), axis=1, keepdims=True
    )
    earlier = jnp.sum(
        jnp.where((owners == own_col) & (lane < sub), 1.0, 0.0), axis=1, keepdims=True
    )
    target = (first_col + 3.0 * earlier)[0:g.W8]
    n = g.dp * ROWS
    pos = lax.broadcasted_iota(I32, (g.W8, n), 1).astype(F32)
    columns = r2[...].reshape(n, g.T)
    return [
        jnp.dot(
            jnp.where(pos == target + float(kind), 1.0, 0.0).astype(BF),
            columns, preferred_element_type=F32,
        ).astype(BF)
        for kind in range(3)
    ]


def per_device(tokens, grad_out, gate_src, up_src, down_src, unit_map, copy_flag):
    g = Geometry(
        lax.axis_size("dp"), lax.axis_size("mp"), tokens.shape[0], tokens.shape[1],
        gate_src.shape[0], unit_map.shape[0],
    )
    X, Z, YC = g.X, g.Z, g.YC
    V = pltpu.VMEM
    dma = pltpu.SemaphoreType.DMA

    def pair(n):
        return [dma((max(n, 1),)), dma((max(n, 1),))]

    scratch = [
        V((2, g.t, g.cols + LANES), F32), V((YC, g.t, g.cols + LANES), F32), V((g.G, g.cols), F32),
        V((Z, YC, LANES), F32), V((1, LANES), I32),
        V((2, Z, X, g.G, g.a), BF), V((2, X, Z, g.G, g.b), BF),
        V(gate_src.shape, BF), V(gate_src.shape, BF), V(gate_src.shape, BF), V((2, 2 * g.R, g.D), BF),
        V((2, LANES, g.T), F32), V((2 * LANES, g.T), BF), V((2, g.T, LANES), BF),
        V((3 * SLOTS * g.dp, 2 * LANES), BF), V((g.dp * ROWS, 2 * LANES), BF),
        V((Z, YC, ROWS, g.T), BF), V((Z, YC, ROWS, g.T), BF), V((YC, Z, ROWS, g.T), BF),
        V((X, Z, g.G, g.a), BF), V((X, Z, g.G, g.b), BF), V((X, Z, g.G, g.a), BF), V((X, Z, g.G, g.b), BF),
        V((X, Z, g.G, g.a), F32), V((Z, g.G, g.b), F32),
        V((g.long, X, g.G, g.a), BF), V((g.long, X, g.G, g.a), BF),
        V((max(g.short, 1), X, g.G, g.a), BF), V((max(g.short, 1), X, g.G, g.a), BF),
        V((X, g.G, g.a), BF), V((X - 1, g.G, g.a), BF),
        V((X - 1, Z, g.G, g.b), BF), V((X - 1, Z, g.G, g.b), BF),
        V((Z, g.G, g.b), BF), V((Z - 1, g.G, g.b), BF), V((Z, g.G, g.b), F32),
        V((YC, g.t, g.cols), F32), V((YC, g.t, g.cols), F32),
        V((g.wide, g.D), BF), V((g.wide, g.D), BF), V((g.wide, g.D), BF),
        dma((3,)), dma((3,)),
    ]
    counts = [YC, Z - 1, X - 1, Z - 1, Z - 1, X - 1, Z, X, Z - 1, YC, X, X, g.long, g.short, X - 1, X - 1, Z - 1, YC]
    for n in counts:
        scratch += pair(n)
    vm = pl.BlockSpec(memory_space=pltpu.VMEM)
    anyw = pl.BlockSpec(memory_space=pl.ANY)
    wide_shape = jax.ShapeDtypeStruct((g.wide, g.D), BF)
    tok_shape = jax.ShapeDtypeStruct(tokens.shape, BF)
    macs = 6 * g.T * g.src * g.D + 3 * g.T * g.wide * g.D
    return pl.pallas_call(
        functools.partial(kernel, g),
        out_shape=(tok_shape, tok_shape, wide_shape, wide_shape, wide_shape),
        in_specs=[vm, vm, anyw, anyw, anyw, vm, vm],
        out_specs=(vm, vm, anyw, anyw, anyw),
        scratch_shapes=scratch,
        compiler_params=pltpu.CompilerParams(
            collective_id=0, has_side_effects=True, vmem_limit_bytes=56 * 1024 * 1024
        ),
        cost_estimate=pl.CostEstimate(
            flops=2 * macs, bytes_accessed=3 * 2 * g.D * (g.src + g.wide), transcendentals=g.T * g.src
        ),
        name="widened_layer",
    )(
        tokens, grad_out, gate_src, up_src, down_src,
        unit_map.reshape(1, -1), copy_flag.reshape(1, -1),
    )


def solution(mesh):
    in_specs = (
        P("dp", "mp"),
        P("dp", "mp"),
        P(("dp", "mp"), None),
        P(("dp", "mp"), None),
        P(("dp", "mp"), None),
        P(("dp", "mp")),
        P(("dp", "mp")),
    )
    out_specs = (
        P("dp", "mp"),
        P("dp", "mp"),
        P(("dp", "mp"), None),
        P(("dp", "mp"), None),
        P(("dp", "mp"), None),
    )
    return jax.shard_map(
        per_device, mesh=mesh, in_specs=in_specs, out_specs=out_specs, check_vma=False
    )
```

time: 800 us -> 81.9 us (0.10)
  blocking collectives: 367 us -> 0 us
  waiting for transfers between devices: 215 us -> 0 us
  other arithmetic: 83.1 us -> 0 us
  Pallas kernels: 0 us -> 74.5 us
  local copies, waits for them, and re-layouts: 80.3 us -> 6.53 us
  starting transfers between devices: 20.9 us -> 0 us
  between operations: 14.9 us -> 0.66 us
  matrix products: 14.1 us -> 0 us
    unnamed x1 -> x0, blocking collectives: 264 us -> none
    all_to_all x3 -> x0, waiting for transfers between devices: 136 us -> none  [the longest x1 72 us: per_device(): lax.all_to_all(down_src[send_idx], 'dp', split_axis=0, concat_axis=0, til...]
    all_gather x3 -> x0, blocking collectives: 102 us -> none  [the longest x1 81.4 us: per_device(): full_packed = lax.all_gather(packed, ('dp', 'mp'), axis=0, tiled=True)]
    scatter-add x1 -> x0, other arithmetic: 80.7 us -> none  [per_device(): jax.ops.segment_sum(full_flag.astype(jnp.float32), full_map, num_segments...]
    reduce_scatter x2 -> x0, waiting for transfers between devices: 79.1 us -> none  [the longest x1 45.1 us: per_device(): lax.psum_scatter(out_part, 'mp', scatter_dimension=1, tiled=True)]
    pallas_call x0 -> x1, Pallas kernels: none -> 74.5 us  [per_device(): pl.pallas_call(functools.partial(kernel, g), out_shape=(tok_shape, tok_sh...]
    all_to_all x6 -> x0, local copies, waits for them, and re-layouts: 32.9 us -> none  [the longest x2 11 us: per_device(): lax.all_to_all(up_src[send_idx], 'dp', split_axis=0, concat_axis=0, tiled...]
    all_to_all x3 -> x0, starting transfers between devices: 20.6 us -> none  [the longest x1 7 us: per_device(): lax.all_to_all(gate_src[send_idx], 'dp', split_axis=0, concat_axis=0, til...]
  transfers between devices with their start and end apart: 7 -> 0, of which waited for: 4 -> 0; matrix products, arithmetic and copies ran while one was open for 15% -> 0% of each run, Pallas kernels for 0% -> 0%
where the time goes in v1:
time: 81.9 us; the launch traced here: 81.7 us
  Pallas kernels  74.5 us (91%)
  local copies, waits for them, and re-layouts  6.53 us (8%)
    pallas_call x1, Pallas kernels, per_device(): pl.pallas_call(functools.partial(kernel, g), out_shape=(tok_shape, tok_sh...  74.5 us
    unnamed x13, local copies, waits for them, and re-layouts  6.53 us

profile of v1, /device:TPU:1, one launch (start us, length us, event | category | flops | bytes accessed | tf_op | source)
XLA Modules:
  0.0 81.7 jit_solution(4223125650693115527)
XLA Ops:
  0.6 74.5 %widened_layer.1 = (bf16[2,1664]{1,0:T(2,128)(2,1)}, bf16[2,1664]{1,0:T(2,128)(2,1)}, bf16[60,6656]{1,0:T(8,128)(2,1)}, bf16[60,6656]{1,0:T(8,128)(2,1)}, bf16[60,6656]{1,0:T(8,128)(2,1)}) custom-call(bf16[2,1664]{1,0:T(2,128)(2,1)} %refs_0_.1, bf16[2,1664]{1,0:T(2,128)(2,1)} %refs_1_.1, bf16[40,6656]{1,0:T(8,128)(2,1)} %refs_2_.1, ...), custom_call_target="tpu_custom_call" | custom-call | flops 715653120 | bytes 3993600 | tf_op jit(solution)/shard_map/widened_layer/pallas_call | solution.py:492
  75.1 0.0 copy-start.3
  75.1 0.7 copy-done.3
  75.8 0.0 copy-start.2
  75.8 0.6 copy.17
  76.4 0.1 copy-done.2
  76.5 0.6 copy.18
  77.1 0.0 copy-start.1
  77.1 2.2 %copy.19 = bf16[60,6656]{1,0:T(8,128)(2,1)} copy(bf16[60,6656]{1,0:T(8,128)(2,1)} %get-tuple-element.12) | data formatting | bytes 1597440
  79.3 0.0 copy-done.1
  79.3 0.0 copy-start
  79.3 0.9 %copy.20 = bf16[60,6656]{1,0:T(8,128)(2,1)} copy(bf16[60,6656]{1,0:T(8,128)(2,1)S(1)} %copy-done.1) | data formatting | bytes 1597440
  80.2 0.6 copy-done
  80.8 0.9 %copy.21 = bf16[60,6656]{1,0:T(8,128)(2,1)} copy(bf16[60,6656]{1,0:T(8,128)(2,1)S(1)} %copy-done) | data formatting | bytes 1597440
Async XLA Ops:
  75.1 0.7 copy-start.3
  75.8 0.7 copy-start.2
  77.1 2.2 %copy-start.1 = (bf16[60,6656]{1,0:T(8,128)(2,1)S(1)}, bf16[60,6656]{1,0:T(8,128)(2,1)}, u32[]{:S(2)}) copy-start(bf16[60,6656]{1,0:T(8,128)(2,1)} %get-tuple-element.13) | copy-start | bytes 2396164
  79.3 1.5 %copy-start = (bf16[60,6656]{1,0:T(8,128)(2,1)S(1)}, bf16[60,6656]{1,0:T(8,128)(2,1)}, u32[]{:S(2)}) copy-start(bf16[60,6656]{1,0:T(8,128)(2,1)} %get-tuple-element.14) | copy-start | bytes 2396164

commit v2 on v1

--- a/solution.py
+++ b/solution.py
@@ -16,7 +16,6 @@
 CHIPS_Y = 4
 SLOTS = 3
 LANES = 128
-ROWS = 16
 
 
 def _mod(v, n):
@@ -44,6 +43,7 @@
         self.W8 = -(-wide // 8) * 8
         self.long = self.Z // 2
         self.short = self.Z - 1 - self.long
+        self.M = -(-(self.YC * 3 * SLOTS) // 16) * 16
 
 
 def kernel(g, *refs):
@@ -53,10 +53,10 @@
         buf_a, buf_b,
         w_gate, w_up, w_down, ws,
         lf, lb, lt,
-        ss, sel, msg, r1, r2,
+        ss, spread, regroup, sel, msg, r1, m2, r2,
         sib_a, sib_b, rcv_a, rcv_b, pa, pb,
         ring_sl, ring_rl, ring_ss, ring_rs, ax_s, ax_r,
-        bx_s, bx_r, bz_s, bz_r, sum_b,
+        b1_s, b1_r, b2_s, b2_r, bd_s, bd_r, bz_s, bz_r,
         fin_s, fin_r,
         g_gate, g_up, g_down,
         w_sem, o_sem,
@@ -64,7 +64,7 @@
         sa_s, sa_r, sb_s, sb_r,
         m1_s, m1_r, m2_s, m2_r,
         ra_s, ra_r, rb_s, rb_r,
-        rl_s, rl_r, rs_s, rs_r, axx_s, axx_r, bxx_s, bxx_r, bzz_s, bzz_r, f_s, f_r,
+        rz_s, rz_r, axx_s, axx_r, bxx_s, bxx_r, bzz_s, bzz_r, f_s, f_r,
     ) = refs[12:]
     X, Y, Z, YC = g.X, g.Y, g.Z, g.YC
     dp = lax.axis_index("dp")
@@ -135,6 +135,7 @@
     for k in range(2):
         s1_src[k, :, g.cols:g.cols + LANES] = jnp.broadcast_to(code_row.astype(F32), (g.t, LANES))
     s1_rcv[yc] = s1_src[c]
+    static_matrices(g, spread, regroup)
 
     pl.semaphore_wait(bar, (X - 1) + (Z - 1) + len(yc_peers))
 
@@ -149,10 +150,76 @@
     buf_a[c, z, x] = block[:, 0:g.a]
     buf_b[c, x, z] = block[:, g.a:g.cols]
 
+    right, left = at_z(_mod(z + step, Z)), at_z(_mod(z - step, Z))
+    a_cols = [x] + [_mod(x - k, X) for k in range(1, X)]
+
+    def slots_at(hop):
+        out = [(hop, _mod(z - hop * step, Z))]
+        if 1 <= hop <= g.short:
+            out.append((g.long + hop, _mod(z + hop * step, Z)))
+        return out
+
+    def a_forward(hop, j):
+        if hop < g.long:
+            ref = buf_a.at[c, _mod(z - hop * step, Z), a_cols[j]]
+            i = hop * X + j
+            send(ref, ref, ga_zs.at[i], ga_zr.at[i], right)
+        if hop < g.short:
+            ref = buf_a.at[c, _mod(z + hop * step, Z), a_cols[j]]
+            i = (g.long + hop) * X + j
+            send(ref, ref, ga_zs.at[i], ga_zr.at[i], left)
+
+    def a_arrive(hop, j):
+        i = (hop - 1) * X + j
+        arrive(buf_a.at[c, _mod(z - hop * step, Z), a_cols[j]], ga_zs.at[i], ga_zr.at[i], sibling)
+        if hop <= g.short:
+            i = (g.long + hop - 1) * X + j
+            arrive(buf_a.at[c, _mod(z + hop * step, Z), a_cols[j]], ga_zs.at[i], ga_zr.at[i], sibling)
+
+    def b_forward(hop):
+        if hop < g.long:
+            ref = buf_b.at[c, x, _mod(z - hop * step, Z)]
+            send(ref, ref, gb_zs.at[hop], gb_zr.at[hop], right)
+        if hop < g.short:
+            ref = buf_b.at[c, x, _mod(z + hop * step, Z)]
+            i = g.long + hop
+            send(ref, ref, gb_zs.at[i], gb_zr.at[i], left)
+
+    def b_arrive(hop):
+        arrive(buf_b.at[c, x, _mod(z - hop * step, Z)], gb_zs.at[hop - 1], gb_zr.at[hop - 1], sibling)
+        if hop <= g.short:
+            i = g.long + hop - 1
+            arrive(buf_b.at[c, x, _mod(z + hop * step, Z)], gb_zs.at[i], gb_zr.at[i], sibling)
+
+    x_up, x_down, x_far = _mod(x + 1, X), _mod(x - 1, X), _mod(x + 2, X)
+
+    def b_across(i, b):
+        ref = buf_b.at[c, x, b]
+        send(ref, ref, gb_xs.at[3 * i], gb_xr.at[3 * i], at_x(x_up))
+        send(ref, ref, gb_xs.at[3 * i + 1], gb_xr.at[3 * i + 1], at_x(x_down))
+
+    def b_pass_on(i, b):
+        arrive(buf_b.at[c, x_down, b], gb_xs.at[3 * i], gb_xr.at[3 * i], sibling)
+        arrive(buf_b.at[c, x_up, b], gb_xs.at[3 * i + 1], gb_xr.at[3 * i + 1], sibling)
+        way = 1 - 2 * lax.rem(b, 2)
+        ref = buf_b.at[c, _mod(x - way, X), b]
+        send(ref, ref, gb_xs.at[3 * i + 2], gb_xr.at[3 * i + 2], at_x(_mod(x + way, X)))
+
+    def b_share(i, b):
+        arrive(buf_b.at[c, x_far, b], gb_xs.at[3 * i + 2], gb_xr.at[3 * i + 2], sibling)
+        ref = buf_b.at[c, :, b]
+        send(ref, ref, sb_s.at[i], sb_r.at[i], sibling)
+
+    def a_share(i, b):
+        ref = buf_a.at[c, b]
+        send(ref, ref, sa_s.at[i], sa_r.at[i], sibling)
+
+    b_forward(0)
     for k in range(1, X):
-        send(buf_a.at[c, z, x], buf_a.at[c, z, x], ga_xs.at[k - 1], ga_xr.at[k - 1], at_x(_mod(x + k, X)))
-    for k in range(1, Z):
-        send(buf_b.at[c, x, z], buf_b.at[c, x, z], gb_zs.at[k - 1], gb_zr.at[k - 1], at_z(_mod(z + k, Z)))
+        ref = buf_a.at[c, z, x]
+        send(ref, ref, ga_xs.at[k - 1], ga_xr.at[k - 1], at_x(_mod(x + k, X)))
+    a_forward(0, 0)
+    b_across(0, z)
     for k in range(1, Z):
         send(codes.at[z], codes.at[z], cz_ss.at[k - 1], cz_rs.at[k - 1], at_z(_mod(z + k, Z)))
 
@@ -168,54 +235,38 @@
     ws[1, 0:g.src, :] = w_gate[...]
     ws[1, g.R:g.R + g.src, :] = w_up[...]
 
-    for k in range(1, X):
+    for k in (1, X - 1, *range(2, X - 1)):
         arrive(buf_a.at[c, z, _mod(x - k, X)], ga_xs.at[k - 1], ga_xr.at[k - 1], sibling)
-
-    def ring_gather(hop):
-        if hop < g.long:
-            b = _mod(z - hop * step, Z)
-            send(buf_a.at[c, b], buf_a.at[c, b], ga_zs.at[hop], ga_zr.at[hop], at_z(_mod(z + step, Z)))
-        if hop < g.short:
-            b = _mod(z + hop * step, Z)
-            i = g.long + hop
-            send(buf_a.at[c, b], buf_a.at[c, b], ga_zs.at[i], ga_zr.at[i], at_z(_mod(z - step, Z)))
-
-    def share_a(b, i):
-        send(buf_a.at[c, b], buf_a.at[c, b], sa_s.at[i], sa_r.at[i], sibling)
-
-    ring_gather(0)
-    share_a(z, 0)
-    for k in range(1, Z):
-        arrive(buf_b.at[c, x, _mod(z - k, Z)], gb_zs.at[k - 1], gb_zr.at[k - 1], sibling)
-    for k in range(1, X):
-        send(buf_b.at[c, x], buf_b.at[c, x], gb_xs.at[k - 1], gb_xr.at[k - 1], at_x(_mod(x + k, X)))
-    send(buf_b.at[c, x], buf_b.at[c, x], sb_s.at[0], sb_r.at[0], sibling)
+        a_forward(0, k)
+    a_share(0, z)
     for hop in range(1, g.long + 1):
-        b = _mod(z - hop * step, Z)
-        arrive(buf_a.at[c, b], ga_zs.at[hop - 1], ga_zr.at[hop - 1], sibling)
-        b2 = _mod(z + hop * step, Z)
-        if hop <= g.short:
-            arrive(buf_a.at[c, b2], ga_zs.at[g.long + hop - 1], ga_zr.at[g.long + hop - 1], sibling)
-        ring_gather(hop)
-        share_a(b, hop)
-        if hop <= g.short:
-            share_a(b2, g.long + hop)
-
+        b_arrive(hop)
+        b_forward(hop)
+        for i, b in slots_at(hop):
+            b_across(i, b)
+        for i, b in slots_at(hop - 1):
+            b_pass_on(i, b)
+        for j in (0, 1, X - 1, *range(2, X - 1)):
+            a_arrive(hop, j)
+            a_forward(hop, j)
+        for i, b in slots_at(hop):
+            a_share(i, b)
+        for i, b in slots_at(hop - 1):
+            b_share(i, b)
         if hop == 1:
             for k in range(1, Z):
                 arrive(codes.at[_mod(z - k, Z)], cz_ss.at[k - 1], cz_rs.at[k - 1], sibling)
-            routing(g, codes, ss, sel, dp * X + x)
-    for k in range(1, X):
-        xx = _mod(x - k, X)
-        arrive(buf_b.at[c, xx], gb_xs.at[k - 1], gb_xr.at[k - 1], sibling)
-        send(buf_b.at[c, xx], buf_b.at[c, xx], sb_s.at[k], sb_r.at[k], sibling)
-
-    for k in range(g.long + 1):
-        arrive(buf_a.at[other, _mod(z + k * step, Z)], sa_s.at[k], sa_r.at[k], sibling)
-    for k in range(1, g.short + 1):
-        arrive(buf_a.at[other, _mod(z - k * step, Z)], sa_s.at[g.long + k], sa_r.at[g.long + k], sibling)
-    for k in range(X):
-        arrive(buf_b.at[other, _mod(x - k, X)], sb_s.at[k], sb_r.at[k], sibling)
+            routing(g, codes, ss, spread, sel, dp * X + x)
+    for i, b in slots_at(g.long):
+        b_pass_on(i, b)
+    for i, b in slots_at(g.long):
+        b_share(i, b)
+
+    for i in range(Z):
+        hop = i if i <= g.long else g.long - i
+        b = _mod(z + hop * step, Z)
+        arrive(buf_a.at[other, b], sa_s.at[i], sa_r.at[i], sibling)
+        arrive(buf_b.at[other, :, b], sb_s.at[i], sb_r.at[i], sibling)
 
     nt = (((1,), (1,)), ((), ()))
 
@@ -249,89 +300,143 @@
     def partial(array, lo, hi):
         return jnp.dot(lt[array][:, 0:2 * g.R], ws[array, :, lo:hi], preferred_element_type=F32)
 
+    def partial_b(array, xx):
+        lo = pl.multiple_of(xx * g.cols + g.a, LANES)
+        v = jnp.dot(lt[array][:, 0:2 * g.R], ws[array, :, pl.ds(lo, g.b)], preferred_element_type=F32)
+        return v.reshape(Z, g.G, g.b)
+
+    def own_a(b, xx):
+        return pa[xx, b] + rcv_a[xx, b].astype(F32)
+
+    def reduce_a(hop, xx):
+        if hop < g.long:
+            v = own_a(_mod(z + (g.long - hop) * step, Z), xx)
+            if hop:
+                i = (hop - 1) * X + xx
+                arrive(ring_rl.at[hop - 1, xx], rz_s.at[i], rz_r.at[i], sibling)
+                v = v + ring_rl[hop - 1, xx].astype(F32)
+            ring_sl[hop, xx] = v.astype(BF)
+            i = hop * X + xx
+            send(ring_sl.at[hop, xx], ring_rl.at[hop, xx], rz_s.at[i], rz_r.at[i], right)
+        if hop < g.short:
+            v = own_a(_mod(z - (g.short - hop) * step, Z), xx)
+            if hop:
+                i = (g.long + hop - 1) * X + xx
+                arrive(ring_rs.at[hop - 1, xx], rz_s.at[i], rz_r.at[i], sibling)
+                v = v + ring_rs[hop - 1, xx].astype(F32)
+            ring_ss[hop, xx] = v.astype(BF)
+            i = (g.long + hop) * X + xx
+            send(ring_ss.at[hop, xx], ring_rs.at[hop, xx], rz_s.at[i], rz_r.at[i], left)
+
+    b_long = [(h, _mod(z + (g.long - h) * step, Z)) for h in range(g.long)]
+    b_short = [(g.long + h, _mod(z - (g.short - h) * step, Z)) for h in range(g.short)]
+    b_own = (Z - 1, z)
+    b_order = []
+    for h in range(g.long):
+        b_order.append(b_long[h])
+        if h < g.short:
+            b_order.append(b_short[h])
+    b_order.append(b_own)
+
+    def way_of(b):
+        return 1 - 2 * lax.rem(b, 2)
+
+    def b_first(i, b):
+        b1_s[i] = pb[x_far, b].astype(BF)
+        send(b1_s.at[i], b1_r.at[i], bxx_s.at[3 * i], bxx_r.at[3 * i], at_x(_mod(x + way_of(b), X)))
+
+    def b_direct(i, b):
+        to = _mod(x - way_of(b), X)
+        bd_s[i] = pb[to, b].astype(BF)
+        send(bd_s.at[i], bd_r.at[i], bxx_s.at[3 * i + 1], bxx_r.at[3 * i + 1], at_x(to))
+
+    def b_second(i, b):
+        to = _mod(x + way_of(b), X)
+        arrive(b1_r.at[i], bxx_s.at[3 * i], bxx_r.at[3 * i], sibling)
+        b2_s[i] = (pb[to, b] + b1_r[i].astype(F32)).astype(BF)
+        send(b2_s.at[i], b2_r.at[i], bxx_s.at[3 * i + 2], bxx_r.at[3 * i + 2], at_x(to))
+
+    def b_sum(i, b):
+        arrive(bd_r.at[i], bxx_s.at[3 * i + 1], bxx_r.at[3 * i + 1], sibling)
+        arrive(b2_r.at[i], bxx_s.at[3 * i + 2], bxx_r.at[3 * i + 2], sibling)
+        return pb[x, b] + bd_r[i].astype(F32) + b2_r[i].astype(F32)
+
+    def reduce_b(hop):
+        for chain, to, n in ((b_long, right, g.long), (b_short, left, g.short)):
+            if hop < n:
+                i, b = chain[hop]
+                v = b_sum(i, b)
+                if hop:
+                    arrive(bz_r.at[i - 1], bzz_s.at[i - 1], bzz_r.at[i - 1], sibling)
+                    v = v + bz_r[i - 1].astype(F32)
+                bz_s[i] = v.astype(BF)
+                send(bz_s.at[i], bz_r.at[i], bzz_s.at[i], bzz_r.at[i], to)
+
     for xx in range(X):
         lo = xx * g.cols
         sib_a[xx] = partial(other, lo, lo + g.a).astype(BF).reshape(Z, g.G, g.a)
         send(sib_a.at[xx], rcv_a.at[xx], ra_s.at[xx], ra_r.at[xx], sibling)
-    for xx in range(X):
-        lo = xx * g.cols
-        sib_b[xx] = partial(other, lo + g.a, lo + g.cols).astype(BF).reshape(Z, g.G, g.b)
-        send(sib_b.at[xx], rcv_b.at[xx], rb_s.at[xx], rb_r.at[xx], sibling)
+    for k in range(X):
+        xx = _mod(x + (2, 1, X - 1, 0)[k], X)
+        sib_b[k] = partial_b(other, xx).astype(BF)
+        send(sib_b.at[k], rcv_b.at[k], rb_s.at[k], rb_r.at[k], sibling)
     for xx in range(X):
         lo = xx * g.cols
         pa[xx] = partial(c, lo, lo + g.a).reshape(Z, g.G, g.a)
-    for xx in range(X):
         arrive(rcv_a.at[xx], ra_s.at[xx], ra_r.at[xx], sibling)
-
-    def own_a(b):
-        return pa[:, b] + rcv_a[:, b].astype(F32)
-
-    def ring_reduce(hop):
-        if hop < g.long:
-            v = own_a(_mod(z + (g.long - hop) * step, Z))
-            if hop:
-                arrive(ring_rl.at[hop - 1], rl_s.at[hop - 1], rl_r.at[hop - 1], sibling)
-                v = v + ring_rl[hop - 1].astype(F32)
-            ring_sl[hop] = v.astype(BF)
-            send(ring_sl.at[hop], ring_rl.at[hop], rl_s.at[hop], rl_r.at[hop], at_z(_mod(z + step, Z)))
-        if hop < g.short:
-            v = own_a(_mod(z - (g.short - hop) * step, Z))
-            if hop:
-                arrive(ring_rs.at[hop - 1], rs_s.at[hop - 1], rs_r.at[hop - 1], sibling)
-                v = v + ring_rs[hop - 1].astype(F32)
-            ring_ss[hop] = v.astype(BF)
-            send(ring_ss.at[hop], ring_rs.at[hop], rs_s.at[hop], rs_r.at[hop], at_z(_mod(z - step, Z)))
-
-    ring_reduce(0)
+        reduce_a(0, xx)
+    for k in range(X):
+        xx = _mod(x + (2, 1, X - 1, 0)[k], X)
+        v = partial_b(c, xx)
+        arrive(rcv_b.at[k], rb_s.at[k], rb_r.at[k], sibling)
+        pb[xx] = v + rcv_b[k].astype(F32)
+        if k == 0:
+            for i, b in b_order:
+                b_first(i, b)
+        if k == 2:
+            for i, b in b_order:
+                b_direct(i, b)
 
     picked = jnp.dot(sel[...], lb[...], preferred_element_type=F32).astype(BF)
-    msg[...] = picked.reshape(Z, YC, ROWS, g.T)
+    msg[...] = picked.reshape(Z, g.M, g.T)
     r1[z] = msg[z]
+
+    for i, b in b_order[0:Z // 2]:
+        b_second(i, b)
+    for xx in range(X):
+        reduce_a(1, xx)
     for k in range(1, Z):
         zz = _mod(z + k, Z)
         send(msg.at[zz], r1.at[z], m1_s.at[k - 1], m1_r.at[k - 1], at_z(zz))
-
-    for k in range(X):
-        xx = _mod(x + k + 1, X)
-        lo = pl.multiple_of(xx * g.cols + g.a, LANES)
-        v = jnp.dot(lt[c][:, 0:2 * g.R], ws[c, :, pl.ds(lo, g.b)], preferred_element_type=F32)
-        arrive(rcv_b.at[xx], rb_s.at[xx], rb_r.at[xx], sibling)
-        v = v.reshape(Z, g.G, g.b) + rcv_b[xx].astype(F32)
-        if k < X - 1:
-            bx_s[k] = v.astype(BF)
-            send(bx_s.at[k], bx_r.at[k], bxx_s.at[k], bxx_r.at[k], at_x(xx))
-        else:
-            pb[...] = v
-
-    for hop in range(1, g.long):
-        ring_reduce(hop)
-
+    for i, b in b_order[Z // 2:]:
+        b_second(i, b)
+    reduce_b(0)
+    for xx in range(X):
+        reduce_a(2, xx)
+    reduce_b(1)
+    for xx in range(X):
+        reduce_a(3, xx)
     for k in range(1, Z):
         arrive(r1.at[_mod(z - k, Z)], m1_s.at[k - 1], m1_r.at[k - 1], sibling)
-    r2[yc] = r1[:, yc]
+    m2[...] = jnp.dot(
+        regroup[...], r1[...].reshape(Z * g.M, g.T), preferred_element_type=F32
+    ).astype(BF).reshape(YC, g.M, g.T)
+    r2[yc] = m2[yc]
     for i, peer, _, _ in yc_peers:
-        send(r1.at[:, peer], r2.at[yc], m2_s.at[i], m2_r.at[i], at_yc(peer))
-
-    for k in range(X - 1):
-        arrive(bx_r.at[k], bxx_s.at[k], bxx_r.at[k], sibling)
-    total_b = pb[...]
-    for k in range(X - 1):
-        total_b = total_b + bx_r[k].astype(F32)
-    sum_b[...] = total_b
-    bz_s[...] = total_b.astype(BF)
-    for k in range(1, Z):
-        zz = _mod(z + k, Z)
-        send(bz_s.at[zz], bz_r.at[k - 1], bzz_s.at[k - 1], bzz_r.at[k - 1], at_z(zz))
-
-    v = own_a(z)
-    if g.long:
-        arrive(ring_rl.at[g.long - 1], rl_s.at[g.long - 1], rl_r.at[g.long - 1], sibling)
-        v = v + ring_rl[g.long - 1].astype(F32)
-    if g.short:
-        arrive(ring_rs.at[g.short - 1], rs_s.at[g.short - 1], rs_r.at[g.short - 1], sibling)
-        v = v + ring_rs[g.short - 1].astype(F32)
-    pa[:, z] = v
-    ax_s[...] = v.astype(BF)
+        send(m2.at[peer], r2.at[yc], m2_s.at[i], m2_r.at[i], at_yc(peer))
+    reduce_b(2)
+    reduce_b(3)
+
+    for xx in range(X):
+        v = own_a(z, xx)
+        i = (g.long - 1) * X + xx
+        arrive(ring_rl.at[g.long - 1, xx], rz_s.at[i], rz_r.at[i], sibling)
+        v = v + ring_rl[g.long - 1, xx].astype(F32)
+        i = (g.long + g.short - 1) * X + xx
+        arrive(ring_rs.at[g.short - 1, xx], rz_s.at[i], rz_r.at[i], sibling)
+        v = v + ring_rs[g.short - 1, xx].astype(F32)
+        pa[xx, z] = v
+        ax_s[xx] = v.astype(BF)
     for k in range(1, X):
         xx = _mod(x + k, X)
         send(ax_s.at[xx], ax_r.at[k - 1], axx_s.at[k - 1], axx_r.at[k - 1], at_x(xx))
@@ -361,10 +466,10 @@
     for k in range(1, X):
         arrive(ax_r.at[k - 1], axx_s.at[k - 1], axx_r.at[k - 1], sibling)
         va = va + ax_r[k - 1].astype(F32)
-    vb = sum_b[z]
-    for k in range(1, Z):
-        arrive(bz_r.at[k - 1], bzz_s.at[k - 1], bzz_r.at[k - 1], sibling)
-        vb = vb + bz_r[k - 1].astype(F32)
+    vb = b_sum(*b_own)
+    for i in (g.long - 1, g.long + g.short - 1):
+        arrive(bz_r.at[i], bzz_s.at[i], bzz_r.at[i], sibling)
+        vb = vb + bz_r[i].astype(F32)
     for k in range(YC):
         fin_s[k, :, 0:g.a] = va[k * g.t:(k + 1) * g.t]
         fin_s[k, :, g.a:g.cols] = vb[k * g.t:(k + 1) * g.t]
@@ -385,7 +490,7 @@
         op.wait_send()
 
 
-def routing(g, codes, ss, sel, flat):
+def routing(g, codes, ss, spread, sel, flat):
     n, Z, YC = g.dp, g.Z, g.YC
     c = codes[...].reshape(n, LANES).astype(I32)
     local = (c >> 1) - flat * g.src
@@ -415,18 +520,34 @@
         ):
             q = k * 3 + kind
             ss[q * n:(q + 1) * n, :] = jnp.where(wide_lane == idx + offset, factor, 0.0).astype(BF)
-    q = 3 * SLOTS
-    row = lax.broadcasted_iota(I32, (n * ROWS, q * n), 0)
-    col = lax.broadcasted_iota(I32, (n * ROWS, q * n), 1)
-    spread = jnp.where(col == (row & (ROWS - 1)) * n + (row >> 4), 1.0, 0.0).astype(BF)
-    sel[...] = jnp.dot(spread, ss[...], preferred_element_type=F32).astype(BF)
+    sel[...] = jnp.dot(spread[...], ss[...], preferred_element_type=F32).astype(BF)
+
+
+def static_matrices(g, spread, regroup):
+    per = 3 * SLOTS
+    n, rows = g.dp, g.Z * g.M
+
+    def parts(groups):
+        row = lax.broadcasted_iota(I32, (rows, 1), 0).astype(F32)
+        block = jnp.floor((row + 0.5) * (1.0 / g.M))
+        rest = row - block * g.M
+        inner = jnp.floor((rest + 0.5) * (1.0 / per))
+        return block, inner, rest - inner * per, rest < float(groups * per)
+
+    block, inner, q, valid = parts(g.YC)
+    want = jnp.where(valid, q * n + block * g.YC + inner, -1.0)
+    col = lax.broadcasted_iota(I32, (rows, per * n), 1).astype(F32)
+    spread[...] = jnp.where(col == want, 1.0, 0.0).astype(BF)
+    want = jnp.where(valid, inner * g.M + block * per + q, -1.0)
+    col = lax.broadcasted_iota(I32, (rows, rows), 1).astype(F32)
+    regroup[...] = jnp.where(col == want, 1.0, 0.0).astype(BF)
 
 
 def widened(g, code_row, r2):
     src = (code_row >> 1).astype(F32)
     owner = jnp.floor((src + 0.5) * (1.0 / (g.src * g.X)))
     zz = jnp.floor((owner + 0.5) * (1.0 / g.YC))
-    first = ((owner - zz * g.YC) * g.Z + zz) * ROWS
+    first = (owner - zz * g.YC) * g.M + zz * (3.0 * SLOTS)
     sub = lax.broadcasted_iota(I32, (LANES, LANES), 0)
     lane = lax.broadcasted_iota(I32, (LANES, LANES), 1)
     owners = jnp.broadcast_to(owner, (LANES, LANES))
@@ -438,7 +559,7 @@
         jnp.where((owners == own_col) & (lane < sub), 1.0, 0.0), axis=1, keepdims=True
     )
     target = (first_col + 3.0 * earlier)[0:g.W8]
-    n = g.dp * ROWS
+    n = g.YC * g.M
     pos = lax.broadcasted_iota(I32, (g.W8, n), 1).astype(F32)
     columns = r2[...].reshape(n, g.T)
     return [
@@ -450,6 +571,15 @@
     ]
 
 
+def hand_over(n, *refs):
+    sem = refs[2 * n]
+    ops = [pltpu.make_async_copy(refs[i], refs[n + i], sem.at[i]) for i in range(n)]
+    for op in ops:
+        op.start()
+    for op in ops:
+        op.wait()
+
+
 def per_device(tokens, grad_out, gate_src, up_src, down_src, unit_map, copy_flag):
     g = Geometry(
         lax.axis_size("dp"), lax.axis_size("mp"), tokens.shape[0], tokens.shape[1],
@@ -468,20 +598,24 @@
         V((2, Z, X, g.G, g.a), BF), V((2, X, Z, g.G, g.b), BF),
         V(gate_src.shape, BF), V(gate_src.shape, BF), V(gate_src.shape, BF), V((2, 2 * g.R, g.D), BF),
         V((2, LANES, g.T), F32), V((2 * LANES, g.T), BF), V((2, g.T, LANES), BF),
-        V((3 * SLOTS * g.dp, 2 * LANES), BF), V((g.dp * ROWS, 2 * LANES), BF),
-        V((Z, YC, ROWS, g.T), BF), V((Z, YC, ROWS, g.T), BF), V((YC, Z, ROWS, g.T), BF),
+        V((3 * SLOTS * g.dp, 2 * LANES), BF), V((Z * g.M, 3 * SLOTS * g.dp), BF), V((Z * g.M, Z * g.M), BF),
+        V((Z * g.M, 2 * LANES), BF),
+        V((Z, g.M, g.T), BF), V((Z, g.M, g.T), BF), V((YC, g.M, g.T), BF), V((YC, g.M, g.T), BF),
         V((X, Z, g.G, g.a), BF), V((X, Z, g.G, g.b), BF), V((X, Z, g.G, g.a), BF), V((X, Z, g.G, g.b), BF),
-        V((X, Z, g.G, g.a), F32), V((Z, g.G, g.b), F32),
+        V((X, Z, g.G, g.a), F32), V((X, Z, g.G, g.b), F32),
         V((g.long, X, g.G, g.a), BF), V((g.long, X, g.G, g.a), BF),
-        V((max(g.short, 1), X, g.G, g.a), BF), V((max(g.short, 1), X, g.G, g.a), BF),
+        V((g.short, X, g.G, g.a), BF), V((g.short, X, g.G, g.a), BF),
         V((X, g.G, g.a), BF), V((X - 1, g.G, g.a), BF),
-        V((X - 1, Z, g.G, g.b), BF), V((X - 1, Z, g.G, g.b), BF),
-        V((Z, g.G, g.b), BF), V((Z - 1, g.G, g.b), BF), V((Z, g.G, g.b), F32),
+        *[V((Z, g.G, g.b), BF) for _ in range(6)],
+        V((Z - 1, g.G, g.b), BF), V((Z - 1, g.G, g.b), BF),
         V((YC, g.t, g.cols), F32), V((YC, g.t, g.cols), F32),
         V((g.wide, g.D), BF), V((g.wide, g.D), BF), V((g.wide, g.D), BF),
         dma((3,)), dma((3,)),
     ]
-    counts = [YC, Z - 1, X - 1, Z - 1, Z - 1, X - 1, Z, X, Z - 1, YC, X, X, g.long, g.short, X - 1, X - 1, Z - 1, YC]
+    counts = [
+        YC, Z - 1, X - 1, (Z - 1) * X, Z - 1, 3 * Z, Z, Z, Z - 1, YC, X, X,
+        (Z - 1) * X, X - 1, 3 * Z, Z - 1, YC,
+    ]
     for n in counts:
         scratch += pair(n)
     vm = pl.BlockSpec(memory_space=pltpu.VMEM)
@@ -489,7 +623,7 @@
     wide_shape = jax.ShapeDtypeStruct((g.wide, g.D), BF)
     tok_shape = jax.ShapeDtypeStruct(tokens.shape, BF)
     macs = 6 * g.T * g.src * g.D + 3 * g.T * g.wide * g.D
-    return pl.pallas_call(
+    results = pl.pallas_call(
         functools.partial(kernel, g),
         out_shape=(tok_shape, tok_shape, wide_shape, wide_shape, wide_shape),
         in_specs=[vm, vm, anyw, anyw, anyw, vm, vm],
@@ -506,6 +640,15 @@
         tokens, grad_out, gate_src, up_src, down_src,
         unit_map.reshape(1, -1), copy_flag.reshape(1, -1),
     )
+    return pl.pallas_call(
+        functools.partial(hand_over, len(results)),
+        out_shape=tuple(jax.ShapeDtypeStruct(r.shape, r.dtype) for r in results),
+        in_specs=[anyw] * len(results),
+        out_specs=(anyw,) * len(results),
+        scratch_shapes=[dma((len(results),))],
+        cost_estimate=pl.CostEstimate(flops=0, bytes_accessed=12 * g.wide * g.D, transcendentals=0),
+        name="hand_over",
+    )(*results)
 
 
 def solution(mesh):

time: 81.9 us -> 156 us (1.90)
  Pallas kernels: 74.5 us -> 155 us
  local copies, waits for them, and re-layouts: 6.53 us -> 0 us
    pallas_call x0 -> x1, Pallas kernels: none -> 79 us  [per_device(): pl.pallas_call(functools.partial(hand_over, len(results)), out_shape=tupl...]
    unnamed x13 -> x0, local copies, waits for them, and re-layouts: 6.53 us -> none
where the time goes in v2:
time: 156 us
  Pallas kernels  155 us (99%)
    pallas_call x1, Pallas kernels, per_device(): pl.pallas_call(functools.partial(hand_over, len(results)), out_shape=tupl...  79 us
    pallas_call x1, Pallas kernels, per_device(): pl.pallas_call(functools.partial(kernel, g), out_shape=(tok_shape, tok_sh...  75.9 us

profile of v2, /device:TPU:1, one launch (start us, length us, event | category | flops | bytes accessed | tf_op | source)
XLA Modules:
  0.0 155.5 jit_solution(10569058061809557736)
XLA Ops:
  0.6 75.9 %widened_layer.1 = (bf16[2,1664]{1,0:T(2,128)(2,1)}, bf16[2,1664]{1,0:T(2,128)(2,1)}, bf16[60,6656]{1,0:T(8,128)(2,1)}, bf16[60,6656]{1,0:T(8,128)(2,1)}, bf16[60,6656]{1,0:T(8,128)(2,1)}) custom-call(bf16[2,1664]{1,0:T(2,128)(2,1)} %refs_0_.1, bf16[2,1664]{1,0:T(2,128)(2,1)} %refs_1_.1, bf16[40,6656]{1,0:T(8,128)(2,1)} %refs_2_.1, ...), custom_call_target="tpu_custom_call" | custom-call | flops 715653120 | bytes 3993600 | tf_op jit(solution)/shard_map/widened_layer/pallas_call | solution.py:626
  76.6 79.0 %hand_over.1 = (bf16[2,1664]{1,0:T(2,128)(2,1)}, bf16[2,1664]{1,0:T(2,128)(2,1)}, bf16[60,6656]{1,0:T(8,128)(2,1)}, bf16[60,6656]{1,0:T(8,128)(2,1)}, bf16[60,6656]{1,0:T(8,128)(2,1)}) custom-call(bf16[2,1664]{1,0:T(2,128)(2,1)} %get-tuple-element.10.refs_0_, bf16[2,1664]{1,0:T(2,128)(2,1)} %get-tuple-element.11.refs_1_, ...), custom_call_target="tpu_custom_call" | custom-call | bytes 4792320 | tf_op jit(solution)/shard_map/hand_over/pallas_call | solution.py:643

commit v3 on v2

--- a/solution.py
+++ b/solution.py
@@ -135,7 +135,6 @@
     for k in range(2):
         s1_src[k, :, g.cols:g.cols + LANES] = jnp.broadcast_to(code_row.astype(F32), (g.t, LANES))
     s1_rcv[yc] = s1_src[c]
-    static_matrices(g, spread, regroup)
 
     pl.semaphore_wait(bar, (X - 1) + (Z - 1) + len(yc_peers))
 
@@ -193,14 +192,19 @@
 
     x_up, x_down, x_far = _mod(x + 1, X), _mod(x - 1, X), _mod(x + 2, X)
 
-    def b_across(i, b):
+    def b_across(i, b, last=False):
         ref = buf_b.at[c, x, b]
+        if last:
+            send(ref, ref, gb_xs.at[3 * i + 2], gb_xr.at[3 * i + 2], at_x(x_far))
         send(ref, ref, gb_xs.at[3 * i], gb_xr.at[3 * i], at_x(x_up))
         send(ref, ref, gb_xs.at[3 * i + 1], gb_xr.at[3 * i + 1], at_x(x_down))
 
-    def b_pass_on(i, b):
+    def b_beside(i, b):
         arrive(buf_b.at[c, x_down, b], gb_xs.at[3 * i], gb_xr.at[3 * i], sibling)
         arrive(buf_b.at[c, x_up, b], gb_xs.at[3 * i + 1], gb_xr.at[3 * i + 1], sibling)
+
+    def b_pass_on(i, b):
+        b_beside(i, b)
         way = 1 - 2 * lax.rem(b, 2)
         ref = buf_b.at[c, _mod(x - way, X), b]
         send(ref, ref, gb_xs.at[3 * i + 2], gb_xr.at[3 * i + 2], at_x(_mod(x + way, X)))
@@ -234,6 +238,7 @@
     ws[0, 0:g.src, :] = w_down[...]
     ws[1, 0:g.src, :] = w_gate[...]
     ws[1, g.R:g.R + g.src, :] = w_up[...]
+    spread_rows(g, spread)
 
     for k in (1, X - 1, *range(2, X - 1)):
         arrive(buf_a.at[c, z, _mod(x - k, X)], ga_xs.at[k - 1], ga_xr.at[k - 1], sibling)
@@ -243,24 +248,27 @@
         b_arrive(hop)
         b_forward(hop)
         for i, b in slots_at(hop):
-            b_across(i, b)
-        for i, b in slots_at(hop - 1):
-            b_pass_on(i, b)
+            b_across(i, b, last=hop == g.long)
         for j in (0, 1, X - 1, *range(2, X - 1)):
             a_arrive(hop, j)
             a_forward(hop, j)
+        for i, b in slots_at(hop - 1):
+            b_pass_on(i, b)
         for i, b in slots_at(hop):
             a_share(i, b)
-        for i, b in slots_at(hop - 1):
+        if hop > 1:
+            for i, b in slots_at(hop - 2):
+                b_share(i, b)
+    for k in range(1, Z):
+        arrive(codes.at[_mod(z - k, Z)], cz_ss.at[k - 1], cz_rs.at[k - 1], sibling)
+    routing(g, codes, ss, dp * X + x)
+    for i, b in slots_at(g.long):
+        b_beside(i, b)
+    for hop in (g.long - 1, g.long):
+        for i, b in slots_at(hop):
             b_share(i, b)
-        if hop == 1:
-            for k in range(1, Z):
-                arrive(codes.at[_mod(z - k, Z)], cz_ss.at[k - 1], cz_rs.at[k - 1], sibling)
-            routing(g, codes, ss, spread, sel, dp * X + x)
-    for i, b in slots_at(g.long):
-        b_pass_on(i, b)
-    for i, b in slots_at(g.long):
-        b_share(i, b)
+    sel[...] = jnp.dot(spread[...], ss[...], preferred_element_type=F32).astype(BF)
+    regroup_rows(g, regroup)
 
     for i in range(Z):
         hop = i if i <= g.long else g.long - i
@@ -372,61 +380,51 @@
                 bz_s[i] = v.astype(BF)
                 send(bz_s.at[i], bz_r.at[i], bzz_s.at[i], bzz_r.at[i], to)
 
+    order = [x_far, x_up, x_down, x]
+    for k, xx in enumerate(order):
+        sib_b[k] = partial_b(other, xx).astype(BF)
+        send(sib_b.at[k], rcv_b.at[k], rb_s.at[k], rb_r.at[k], sibling)
     for xx in range(X):
         lo = xx * g.cols
         sib_a[xx] = partial(other, lo, lo + g.a).astype(BF).reshape(Z, g.G, g.a)
         send(sib_a.at[xx], rcv_a.at[xx], ra_s.at[xx], ra_r.at[xx], sibling)
-    for k in range(X):
-        xx = _mod(x + (2, 1, X - 1, 0)[k], X)
-        sib_b[k] = partial_b(other, xx).astype(BF)
-        send(sib_b.at[k], rcv_b.at[k], rb_s.at[k], rb_r.at[k], sibling)
+
+    def chip_b(k):
+        v = partial_b(c, order[k])
+        arrive(rcv_b.at[k], rb_s.at[k], rb_r.at[k], sibling)
+        pb[order[k]] = v + rcv_b[k].astype(F32)
+
+    chip_b(0)
+    for i, b in b_order:
+        b_first(i, b)
+    chip_b(1)
+    chip_b(2)
+    for i, b in b_order:
+        b_direct(i, b)
     for xx in range(X):
         lo = xx * g.cols
         pa[xx] = partial(c, lo, lo + g.a).reshape(Z, g.G, g.a)
         arrive(rcv_a.at[xx], ra_s.at[xx], ra_r.at[xx], sibling)
         reduce_a(0, xx)
-    for k in range(X):
-        xx = _mod(x + (2, 1, X - 1, 0)[k], X)
-        v = partial_b(c, xx)
-        arrive(rcv_b.at[k], rb_s.at[k], rb_r.at[k], sibling)
-        pb[xx] = v + rcv_b[k].astype(F32)
-        if k == 0:
-            for i, b in b_order:
-                b_first(i, b)
-        if k == 2:
-            for i, b in b_order:
-                b_direct(i, b)
+    for i, b in b_order:
+        b_second(i, b)
+    chip_b(3)
+    for xx in range(X):
+        reduce_a(1, xx)
+    reduce_b(0)
 
     picked = jnp.dot(sel[...], lb[...], preferred_element_type=F32).astype(BF)
     msg[...] = picked.reshape(Z, g.M, g.T)
     r1[z] = msg[z]
-
-    for i, b in b_order[0:Z // 2]:
-        b_second(i, b)
-    for xx in range(X):
-        reduce_a(1, xx)
+    for xx in range(X):
+        reduce_a(2, xx)
+    reduce_b(1)
     for k in range(1, Z):
         zz = _mod(z + k, Z)
         send(msg.at[zz], r1.at[z], m1_s.at[k - 1], m1_r.at[k - 1], at_z(zz))
-    for i, b in b_order[Z // 2:]:
-        b_second(i, b)
-    reduce_b(0)
-    for xx in range(X):
-        reduce_a(2, xx)
-    reduce_b(1)
     for xx in range(X):
         reduce_a(3, xx)
-    for k in range(1, Z):
-        arrive(r1.at[_mod(z - k, Z)], m1_s.at[k - 1], m1_r.at[k - 1], sibling)
-    m2[...] = jnp.dot(
-        regroup[...], r1[...].reshape(Z * g.M, g.T), preferred_element_type=F32
-    ).astype(BF).reshape(YC, g.M, g.T)
-    r2[yc] = m2[yc]
-    for i, peer, _, _ in yc_peers:
-        send(m2.at[peer], r2.at[yc], m2_s.at[i], m2_r.at[i], at_yc(peer))
     reduce_b(2)
-    reduce_b(3)
-
     for xx in range(X):
         v = own_a(z, xx)
         i = (g.long - 1) * X + xx
@@ -440,6 +438,30 @@
     for k in range(1, X):
         xx = _mod(x + k, X)
         send(ax_s.at[xx], ax_r.at[k - 1], axx_s.at[k - 1], axx_r.at[k - 1], at_x(xx))
+    reduce_b(3)
+    for k in range(1, Z):
+        arrive(r1.at[_mod(z - k, Z)], m1_s.at[k - 1], m1_r.at[k - 1], sibling)
+    m2[...] = jnp.dot(
+        regroup[...], r1[...].reshape(Z * g.M, g.T), preferred_element_type=F32
+    ).astype(BF).reshape(YC, g.M, g.T)
+    r2[yc] = m2[yc]
+    for i, peer, _, _ in yc_peers:
+        send(m2.at[peer], r2.at[yc], m2_s.at[i], m2_r.at[i], at_yc(peer))
+
+    va = pa[x, z]
+    for k in range(1, X):
+        arrive(ax_r.at[k - 1], axx_s.at[k - 1], axx_r.at[k - 1], sibling)
+        va = va + ax_r[k - 1].astype(F32)
+    vb = b_sum(*b_own)
+    for i in (g.long - 1, g.long + g.short - 1):
+        arrive(bz_r.at[i], bzz_s.at[i], bzz_r.at[i], sibling)
+        vb = vb + bz_r[i].astype(F32)
+    for k in range(YC):
+        fin_s[k, :, 0:g.a] = va[k * g.t:(k + 1) * g.t]
+        fin_s[k, :, g.a:g.cols] = vb[k * g.t:(k + 1) * g.t]
+    fin_r[yc] = fin_s[yc]
+    for i, peer, _, _ in yc_peers:
+        send(fin_s.at[peer], fin_r.at[yc], f_s.at[i], f_r.at[i], at_yc(peer))
 
     for i, _, _, origin in yc_peers:
         arrive(r2.at[origin], m2_s.at[i], m2_r.at[i], sibling)
@@ -462,20 +484,6 @@
     for op in stores:
         op.start()
 
-    va = pa[x, z]
-    for k in range(1, X):
-        arrive(ax_r.at[k - 1], axx_s.at[k - 1], axx_r.at[k - 1], sibling)
-        va = va + ax_r[k - 1].astype(F32)
-    vb = b_sum(*b_own)
-    for i in (g.long - 1, g.long + g.short - 1):
-        arrive(bz_r.at[i], bzz_s.at[i], bzz_r.at[i], sibling)
-        vb = vb + bz_r[i].astype(F32)
-    for k in range(YC):
-        fin_s[k, :, 0:g.a] = va[k * g.t:(k + 1) * g.t]
-        fin_s[k, :, g.a:g.cols] = vb[k * g.t:(k + 1) * g.t]
-    fin_r[yc] = fin_s[yc]
-    for i, peer, _, _ in yc_peers:
-        send(fin_s.at[peer], fin_r.at[yc], f_s.at[i], f_r.at[i], at_yc(peer))
     for i, _, _, origin in yc_peers:
         arrive(fin_r.at[origin], f_s.at[i], f_r.at[i], sibling)
     for k, out in enumerate((o_out, o_in)):
@@ -490,7 +498,7 @@
         op.wait_send()
 
 
-def routing(g, codes, ss, spread, sel, flat):
+def routing(g, codes, ss, flat):
     n, Z, YC = g.dp, g.Z, g.YC
     c = codes[...].reshape(n, LANES).astype(I32)
     local = (c >> 1) - flat * g.src
@@ -520,26 +528,28 @@
         ):
             q = k * 3 + kind
             ss[q * n:(q + 1) * n, :] = jnp.where(wide_lane == idx + offset, factor, 0.0).astype(BF)
-    sel[...] = jnp.dot(spread[...], ss[...], preferred_element_type=F32).astype(BF)
-
-
-def static_matrices(g, spread, regroup):
+
+
+def row_parts(g, groups):
     per = 3 * SLOTS
-    n, rows = g.dp, g.Z * g.M
-
-    def parts(groups):
-        row = lax.broadcasted_iota(I32, (rows, 1), 0).astype(F32)
-        block = jnp.floor((row + 0.5) * (1.0 / g.M))
-        rest = row - block * g.M
-        inner = jnp.floor((rest + 0.5) * (1.0 / per))
-        return block, inner, rest - inner * per, rest < float(groups * per)
-
-    block, inner, q, valid = parts(g.YC)
-    want = jnp.where(valid, q * n + block * g.YC + inner, -1.0)
-    col = lax.broadcasted_iota(I32, (rows, per * n), 1).astype(F32)
+    row = lax.broadcasted_iota(I32, (g.Z * g.M, 1), 0).astype(F32)
+    block = jnp.floor((row + 0.5) * (1.0 / g.M))
+    rest = row - block * g.M
+    inner = jnp.floor((rest + 0.5) * (1.0 / per))
+    return block, inner, rest - inner * per, rest < float(groups * per)
+
+
+def spread_rows(g, spread):
+    block, inner, q, valid = row_parts(g, g.YC)
+    want = jnp.where(valid, q * g.dp + block * g.YC + inner, -1.0)
+    col = lax.broadcasted_iota(I32, spread.shape, 1).astype(F32)
     spread[...] = jnp.where(col == want, 1.0, 0.0).astype(BF)
-    want = jnp.where(valid, inner * g.M + block * per + q, -1.0)
-    col = lax.broadcasted_iota(I32, (rows, rows), 1).astype(F32)
+
+
+def regroup_rows(g, regroup):
+    block, inner, q, valid = row_parts(g, g.Z)
+    want = jnp.where(valid, inner * g.M + block * (3.0 * SLOTS) + q, -1.0)
+    col = lax.broadcasted_iota(I32, regroup.shape, 1).astype(F32)
     regroup[...] = jnp.where(col == want, 1.0, 0.0).astype(BF)
 
 
@@ -571,13 +581,28 @@
     ]
 
 
+PARTS = 4
+
+
 def hand_over(n, *refs):
-    sem = refs[2 * n]
-    ops = [pltpu.make_async_copy(refs[i], refs[n + i], sem.at[i]) for i in range(n)]
-    for op in ops:
-        op.start()
-    for op in ops:
-        op.wait()
+    ins, outs, bufs, (sem_in, sem_out) = refs[:n], refs[n:2 * n], refs[2 * n:3 * n], refs[3 * n:]
+    steps = []
+    for i in range(n):
+        cols = ins[i].shape[1]
+        width = cols // PARTS if cols % (PARTS * LANES) == 0 else cols
+        for lo in range(0, cols, width):
+            k, part = len(steps), (slice(None), pl.ds(lo, width))
+            steps.append((
+                pltpu.make_async_copy(ins[i].at[part], bufs[i].at[part], sem_in.at[k]),
+                pltpu.make_async_copy(bufs[i].at[part], outs[i].at[part], sem_out.at[k]),
+            ))
+    for fetch, _ in steps:
+        fetch.start()
+    for fetch, store in steps:
+        fetch.wait()
+        store.start()
+    for _, store in steps:
+        store.wait()
 
 
 def per_device(tokens, grad_out, gate_src, up_src, down_src, unit_map, copy_flag):
@@ -645,7 +670,7 @@
         out_shape=tuple(jax.ShapeDtypeStruct(r.shape, r.dtype) for r in results),
         in_specs=[anyw] * len(results),
         out_specs=(anyw,) * len(results),
-        scratch_shapes=[dma((len(results),))],
+        scratch_shapes=[V(r.shape, r.dtype) for r in results] + [dma((len(results) * PARTS,))] * 2,
         cost_estimate=pl.CostEstimate(flops=0, bytes_accessed=12 * g.wide * g.D, transcendentals=0),
         name="hand_over",
     )(*results)

time: 156 us -> 76.6 us (0.49)
  Pallas kernels: 155 us -> 75.8 us
    pallas_call x1, Pallas kernels: 79 us -> 2.88 us  [per_device(): pl.pallas_call(functools.partial(hand_over, len(results)), out_shape=tupl...]
    pallas_call x1, Pallas kernels: 75.9 us -> 72.9 us  [per_device(): pl.pallas_call(functools.partial(kernel, g), out_shape=(tok_shape, tok_sh...]
where the time goes in v3:
time: 76.6 us; the launch traced here: 76.4 us
  Pallas kernels  75.8 us (99%)
    pallas_call x1, Pallas kernels, per_device(): pl.pallas_call(functools.partial(kernel, g), out_shape=(tok_shape, tok_sh...  72.9 us
    pallas_call x1, Pallas kernels, per_device(): pl.pallas_call(functools.partial(hand_over, len(results)), out_shape=tupl...  2.88 us

profile of v3, /device:TPU:1, one launch (start us, length us, event | category | flops | bytes accessed | tf_op | source)
XLA Modules:
  0.0 76.4 jit_solution(1032819079339794882)
XLA Ops:
  0.6 72.9 %widened_layer.1 = (bf16[2,1664]{1,0:T(2,128)(2,1)}, bf16[2,1664]{1,0:T(2,128)(2,1)}, bf16[60,6656]{1,0:T(8,128)(2,1)}, bf16[60,6656]{1,0:T(8,128)(2,1)}, bf16[60,6656]{1,0:T(8,128)(2,1)}) custom-call(bf16[2,1664]{1,0:T(2,128)(2,1)} %refs_0_.1, bf16[2,1664]{1,0:T(2,128)(2,1)} %refs_1_.1, bf16[40,6656]{1,0:T(8,128)(2,1)} %refs_2_.1, ...), custom_call_target="tpu_custom_call" | custom-call | flops 715653120 | bytes 3993600 | tf_op jit(solution)/shard_map/widened_layer/pallas_call | solution.py:651
  73.6 2.9 %hand_over.1 = (bf16[2,1664]{1,0:T(2,128)(2,1)}, bf16[2,1664]{1,0:T(2,128)(2,1)}, bf16[60,6656]{1,0:T(8,128)(2,1)}, bf16[60,6656]{1,0:T(8,128)(2,1)}, bf16[60,6656]{1,0:T(8,128)(2,1)}) custom-call(bf16[2,1664]{1,0:T(2,128)(2,1)} %get-tuple-element.10.refs_0_, bf16[2,1664]{1,0:T(2,128)(2,1)} %get-tuple-element.11.refs_1_, ...), custom_call_target="tpu_custom_call" | custom-call | bytes 4792320 | tf_op jit(solution)/shard_map/hand_over/pallas_call | solution.py:668

commit v4 on v3

--- a/solution.py
+++ b/solution.py
@@ -51,10 +51,10 @@
     (
         s1_src, s1_rcv, asm, codes, own_code,
         buf_a, buf_b,
-        w_gate, w_up, w_down, ws,
-        lf, lb, lt,
+        w_own, w_out, ws,
+        pre_s, pre_r, lf, lb, lt,
         ss, spread, regroup, sel, msg, r1, m2, r2,
-        sib_a, sib_b, rcv_a, rcv_b, pa, pb,
+        pa, pb,
         ring_sl, ring_rl, ring_ss, ring_rs, ax_s, ax_r,
         b1_s, b1_r, b2_s, b2_r, bd_s, bd_r, bz_s, bz_r,
         fin_s, fin_r,
@@ -63,7 +63,7 @@
         s1_ss, s1_rs, cz_ss, cz_rs, ga_xs, ga_xr, ga_zs, ga_zr, gb_zs, gb_zr, gb_xs, gb_xr,
         sa_s, sa_r, sb_s, sb_r,
         m1_s, m1_r, m2_s, m2_r,
-        ra_s, ra_r, rb_s, rb_r,
+        wx_s, wx_r, px_s, px_r,
         rz_s, rz_r, axx_s, axx_r, bxx_s, bxx_r, bzz_s, bzz_r, f_s, f_r,
     ) = refs[12:]
     X, Y, Z, YC = g.X, g.Y, g.Z, g.YC
@@ -120,8 +120,8 @@
         pl.semaphore_signal(bar, inc=1, device_id=at_yc(peer), device_id_type=MESH)
 
     loads = [
-        pltpu.make_async_copy(h, v, w_sem.at[i])
-        for i, (h, v) in enumerate(((gate_h, w_gate), (up_h, w_up), (down_h, w_down)))
+        pltpu.make_async_copy(h, w_own.at[i], w_sem.at[i])
+        for i, h in enumerate((gate_h, up_h, down_h))
     ]
     for op in loads:
         op.start()
@@ -229,15 +229,19 @@
 
     for op in loads:
         op.wait()
-    ws[0, g.R:2 * g.R, :] = jnp.zeros((g.R, g.D), BF)
     if g.R > g.src:
         pad = jnp.zeros((16, g.D), BF)
-        ws[0, g.R - 16:g.R, :] = pad
-        ws[1, g.R - 16:g.R, :] = pad
-        ws[1, 2 * g.R - 16:2 * g.R, :] = pad
-    ws[0, 0:g.src, :] = w_down[...]
-    ws[1, 0:g.src, :] = w_gate[...]
-    ws[1, g.R:g.R + g.src, :] = w_up[...]
+        w_out[0, g.R - 16:g.R, :] = pad
+        w_out[1, g.R - 16:g.R, :] = pad
+        ws[g.R - 16:g.R, :] = pad
+        ws[3 * g.R - 16:3 * g.R, :] = pad
+    w_out[0, 0:g.src, :] = w_own[2 * other]
+    w_out[1, 0:g.src, :] = w_own[1]
+    for k in range(2):
+        rows = ws.at[pl.ds((2 * k + 1) * g.R, g.R)]
+        send(w_out.at[k], rows, wx_s.at[k], wx_r.at[k], sibling)
+    ws[0:g.src, :] = w_own[2 * c]
+    ws[2 * g.R:2 * g.R + g.src, :] = w_own[1]
     spread_rows(g, spread)
 
     for k in (1, X - 1, *range(2, X - 1)):
@@ -270,12 +274,6 @@
     sel[...] = jnp.dot(spread[...], ss[...], preferred_element_type=F32).astype(BF)
     regroup_rows(g, regroup)
 
-    for i in range(Z):
-        hop = i if i <= g.long else g.long - i
-        b = _mod(z + hop * step, Z)
-        arrive(buf_a.at[other, b], sa_s.at[i], sa_r.at[i], sibling)
-        arrive(buf_b.at[other, :, b], sb_s.at[i], sb_r.at[i], sibling)
-
     nt = (((1,), (1,)), ((), ()))
 
     def rows_a(array, xx):
@@ -284,37 +282,46 @@
     def rows_b(array, xx):
         return buf_b[array, xx].reshape(g.T, g.b)
 
-    pre = jnp.zeros((2 * g.R, g.T), F32)
-    gh = jnp.zeros((g.R, g.T), F32)
+    for k in range(2):
+        rows = ws.at[pl.ds((2 * k + 1) * g.R, g.R)]
+        arrive(rows, wx_s.at[k], wx_r.at[k], sibling)
+    pre = jnp.zeros((4 * g.R, g.T), F32)
     for xx in range(X):
         lo, mid, hi = xx * g.cols, xx * g.cols + g.a, (xx + 1) * g.cols
-        pre += lax.dot_general(ws[1, :, lo:mid], rows_a(0, xx), nt, preferred_element_type=F32)
-        pre += lax.dot_general(ws[1, :, mid:hi], rows_b(0, xx), nt, preferred_element_type=F32)
-        gh += lax.dot_general(ws[0, 0:g.R, lo:mid], rows_a(1, xx), nt, preferred_element_type=F32)
-        gh += lax.dot_general(ws[0, 0:g.R, mid:hi], rows_b(1, xx), nt, preferred_element_type=F32)
-    pre_gate = pre[0:g.src]
-    pre_up = pre[g.R:g.R + g.src]
-    gh = gh[0:g.src]
+        pre += lax.dot_general(ws[:, lo:mid], rows_a(c, xx), nt, preferred_element_type=F32)
+        pre += lax.dot_general(ws[:, mid:hi], rows_b(c, xx), nt, preferred_element_type=F32)
+    pre_s[...] = pre
+    send(pre_s, pre_r, px_s.at[0], px_r.at[0], sibling)
+    arrive(pre_r, px_s.at[0], px_r.at[0], sibling)
+
+    def turned(lo):
+        return jnp.concatenate([pre_r[lo + g.R:lo + 2 * g.R], pre_r[lo:lo + g.R]], axis=0)
+
+    first = c == 0
+    pre_gate = jnp.where(first, pre_s[0:2 * g.R], turned(0))
+    pre_up = jnp.where(first, pre_s[2 * g.R:4 * g.R], turned(2 * g.R))
+    gh = jnp.where(first, turned(0), pre_s[0:2 * g.R])
     sigma = jax.nn.sigmoid(pre_gate)
     active = pre_gate * sigma
+    hidden = active * pre_up
+    d_gate = gh * pre_up * (sigma + active * (1.0 - sigma))
+    d_up = gh * active
     lf[...] = jnp.zeros(lf.shape, F32)
-    lf[0, 0:g.src, :] = active * pre_up
-    lf[1, 0:g.src, :] = gh * pre_up * (sigma + active * (1.0 - sigma))
-    lf[1, g.R:g.R + g.src, :] = gh * active
+    lf[0:2 * g.R, :] = jnp.where(first, d_gate, hidden)
+    lf[2 * g.R:4 * g.R, :] = jnp.where(first, d_up, 0.0)
     for k in range(2):
-        lb[k * LANES:(k + 1) * LANES, :] = lf[k].astype(BF)
-        lt[k] = lf[k].T.astype(BF)
-
-    def partial(array, lo, hi):
-        return jnp.dot(lt[array][:, 0:2 * g.R], ws[array, :, lo:hi], preferred_element_type=F32)
-
-    def partial_b(array, xx):
-        lo = pl.multiple_of(xx * g.cols + g.a, LANES)
-        v = jnp.dot(lt[array][:, 0:2 * g.R], ws[array, :, pl.ds(lo, g.b)], preferred_element_type=F32)
-        return v.reshape(Z, g.G, g.b)
+        lt[:, k * LANES:(k + 1) * LANES] = lf[k * LANES:(k + 1) * LANES, :].T.astype(BF)
+    lf[...] = jnp.zeros(lf.shape, F32)
+    lf[0:g.R, :] = hidden[0:g.R]
+    lf[LANES:LANES + g.R, :] = d_gate[0:g.R]
+    lf[LANES + g.R:LANES + 2 * g.R, :] = d_up[0:g.R]
+    lb[...] = lf[...].astype(BF)
+
+    def partial(lo, width):
+        return jnp.dot(lt[:, 0:4 * g.R], ws[:, pl.ds(lo, width)], preferred_element_type=F32)
 
     def own_a(b, xx):
-        return pa[xx, b] + rcv_a[xx, b].astype(F32)
+        return pa[xx, b]
 
     def reduce_a(hop, xx):
         if hop < g.long:
@@ -381,18 +388,10 @@
                 send(bz_s.at[i], bz_r.at[i], bzz_s.at[i], bzz_r.at[i], to)
 
     order = [x_far, x_up, x_down, x]
-    for k, xx in enumerate(order):
-        sib_b[k] = partial_b(other, xx).astype(BF)
-        send(sib_b.at[k], rcv_b.at[k], rb_s.at[k], rb_r.at[k], sibling)
-    for xx in range(X):
-        lo = xx * g.cols
-        sib_a[xx] = partial(other, lo, lo + g.a).astype(BF).reshape(Z, g.G, g.a)
-        send(sib_a.at[xx], rcv_a.at[xx], ra_s.at[xx], ra_r.at[xx], sibling)
 
     def chip_b(k):
-        v = partial_b(c, order[k])
-        arrive(rcv_b.at[k], rb_s.at[k], rb_r.at[k], sibling)
-        pb[order[k]] = v + rcv_b[k].astype(F32)
+        lo = pl.multiple_of(order[k] * g.cols + g.a, LANES)
+        pb[order[k]] = partial(lo, g.b).reshape(Z, g.G, g.b)
 
     chip_b(0)
     for i, b in b_order:
@@ -402,9 +401,7 @@
     for i, b in b_order:
         b_direct(i, b)
     for xx in range(X):
-        lo = xx * g.cols
-        pa[xx] = partial(c, lo, lo + g.a).reshape(Z, g.G, g.a)
-        arrive(rcv_a.at[xx], ra_s.at[xx], ra_r.at[xx], sibling)
+        pa[xx] = partial(xx * g.cols, g.a).reshape(Z, g.G, g.a)
         reduce_a(0, xx)
     for i, b in b_order:
         b_second(i, b)
@@ -463,6 +460,12 @@
     for i, peer, _, _ in yc_peers:
         send(fin_s.at[peer], fin_r.at[yc], f_s.at[i], f_r.at[i], at_yc(peer))
 
+    for i in range(Z):
+        hop = i if i <= g.long else g.long - i
+        b = _mod(z + hop * step, Z)
+        arrive(buf_a.at[other, b], sa_s.at[i], sa_r.at[i], sibling)
+        arrive(buf_b.at[other, :, b], sb_s.at[i], sb_r.at[i], sibling)
+
     for i, _, _, origin in yc_peers:
         arrive(r2.at[origin], m2_s.at[i], m2_r.at[i], sibling)
     wide = widened(g, own_code[...], r2)
@@ -484,9 +487,11 @@
     for op in stores:
         op.start()
 
+    for op in sent:
+        op.wait_send()
     for i, _, _, origin in yc_peers:
         arrive(fin_r.at[origin], f_s.at[i], f_r.at[i], sibling)
-    for k, out in enumerate((o_out, o_in)):
+    for k, out in enumerate((o_in, o_out)):
         total = fin_r[k]
         for yy in range(1, Y):
             total = total + fin_r[yy * CORES + k]
@@ -494,8 +499,6 @@
 
     for op in stores:
         op.wait()
-    for op in sent:
-        op.wait_send()
 
 
 def routing(g, codes, ss, flat):
@@ -621,12 +624,12 @@
         V((2, g.t, g.cols + LANES), F32), V((YC, g.t, g.cols + LANES), F32), V((g.G, g.cols), F32),
         V((Z, YC, LANES), F32), V((1, LANES), I32),
         V((2, Z, X, g.G, g.a), BF), V((2, X, Z, g.G, g.b), BF),
-        V(gate_src.shape, BF), V(gate_src.shape, BF), V(gate_src.shape, BF), V((2, 2 * g.R, g.D), BF),
-        V((2, LANES, g.T), F32), V((2 * LANES, g.T), BF), V((2, g.T, LANES), BF),
+        V((3, *gate_src.shape), BF), V((2, g.R, g.D), BF), V((4 * g.R, g.D), BF),
+        V((4 * g.R, g.T), F32), V((4 * g.R, g.T), F32),
+        V((2 * LANES, g.T), F32), V((2 * LANES, g.T), BF), V((g.T, 2 * LANES), BF),
         V((3 * SLOTS * g.dp, 2 * LANES), BF), V((Z * g.M, 3 * SLOTS * g.dp), BF), V((Z * g.M, Z * g.M), BF),
         V((Z * g.M, 2 * LANES), BF),
         V((Z, g.M, g.T), BF), V((Z, g.M, g.T), BF), V((YC, g.M, g.T), BF), V((YC, g.M, g.T), BF),
-        V((X, Z, g.G, g.a), BF), V((X, Z, g.G, g.b), BF), V((X, Z, g.G, g.a), BF), V((X, Z, g.G, g.b), BF),
         V((X, Z, g.G, g.a), F32), V((X, Z, g.G, g.b), F32),
         V((g.long, X, g.G, g.a), BF), V((g.long, X, g.G, g.a), BF),
         V((g.short, X, g.G, g.a), BF), V((g.short, X, g.G, g.a), BF),
@@ -638,7 +641,7 @@
         dma((3,)), dma((3,)),
     ]
     counts = [
-        YC, Z - 1, X - 1, (Z - 1) * X, Z - 1, 3 * Z, Z, Z, Z - 1, YC, X, X,
+        YC, Z - 1, X - 1, (Z - 1) * X, Z - 1, 3 * Z, Z, Z, Z - 1, YC, 2, 1,
         (Z - 1) * X, X - 1, 3 * Z, Z - 1, YC,
     ]
     for n in counts:

time: 76.6 us -> 74.5 us (0.973)
  Pallas kernels: 75.8 us -> 73.7 us
    pallas_call x1, Pallas kernels: 72.9 us -> 70.8 us  [per_device(): pl.pallas_call(functools.partial(kernel, g), out_shape=(tok_shape, tok_sh...]
where the time goes in v4:
time: 74.5 us; the launch traced here: 74.3 us
  Pallas kernels  73.7 us (99%)
    pallas_call x1, Pallas kernels, per_device(): pl.pallas_call(functools.partial(kernel, g), out_shape=(tok_shape, tok_sh...  70.8 us
    pallas_call x1, Pallas kernels, per_device(): pl.pallas_call(functools.partial(hand_over, len(results)), out_shape=tupl...  2.88 us

profile of v4, /device:TPU:1, one launch (start us, length us, event | category | flops | bytes accessed | tf_op | source)
XLA Modules:
  0.0 74.3 jit_solution(14760968624928316156)
XLA Ops:
  0.6 70.8 %widened_layer.1 = (bf16[2,1664]{1,0:T(2,128)(2,1)}, bf16[2,1664]{1,0:T(2,128)(2,1)}, bf16[60,6656]{1,0:T(8,128)(2,1)}, bf16[60,6656]{1,0:T(8,128)(2,1)}, bf16[60,6656]{1,0:T(8,128)(2,1)}) custom-call(bf16[2,1664]{1,0:T(2,128)(2,1)} %refs_0_.1, bf16[2,1664]{1,0:T(2,128)(2,1)} %refs_1_.1, bf16[40,6656]{1,0:T(8,128)(2,1)} %refs_2_.1, ...), custom_call_target="tpu_custom_call" | custom-call | flops 715653120 | bytes 3993600 | tf_op jit(solution)/shard_map/widened_layer/pallas_call | solution.py:654
  71.4 2.9 %hand_over.1 = (bf16[2,1664]{1,0:T(2,128)(2,1)}, bf16[2,1664]{1,0:T(2,128)(2,1)}, bf16[60,6656]{1,0:T(8,128)(2,1)}, bf16[60,6656]{1,0:T(8,128)(2,1)}, bf16[60,6656]{1,0:T(8,128)(2,1)}) custom-call(bf16[2,1664]{1,0:T(2,128)(2,1)} %get-tuple-element.10.refs_0_, bf16[2,1664]{1,0:T(2,128)(2,1)} %get-tuple-element.11.refs_1_, ...), custom_call_target="tpu_custom_call" | custom-call | bytes 4792320 | tf_op jit(solution)/shard_map/hand_over/pallas_call | solution.py:671

commit v5 on v4

--- a/solution.py
+++ b/solution.py
@@ -36,6 +36,8 @@
         tiles = cols // LANES
         self.a = (tiles // 2) * LANES
         self.b = cols - self.a
+        self.ra = (tiles // 2 + 1) * LANES
+        self.rb = cols - self.ra
         self.D = cols * n_mp
         self.src = src
         self.R = -(-src // 16) * 16
@@ -390,9 +392,12 @@
     order = [x_far, x_up, x_down, x]
 
     def chip_b(k):
-        lo = pl.multiple_of(order[k] * g.cols + g.a, LANES)
-        pb[order[k]] = partial(lo, g.b).reshape(Z, g.G, g.b)
-
+        lo = pl.multiple_of(order[k] * g.cols + g.ra, LANES)
+        pb[order[k]] = partial(lo, g.rb).reshape(Z, g.G, g.rb)
+
+    picked = jnp.dot(sel[...], lb[...], preferred_element_type=F32).astype(BF)
+    msg[...] = picked.reshape(Z, g.M, g.T)
+    r1[z] = msg[z]
     chip_b(0)
     for i, b in b_order:
         b_first(i, b)
@@ -401,27 +406,36 @@
     for i, b in b_order:
         b_direct(i, b)
     for xx in range(X):
-        pa[xx] = partial(xx * g.cols, g.a).reshape(Z, g.G, g.a)
+        pa[xx] = partial(xx * g.cols, g.ra).reshape(Z, g.G, g.ra)
         reduce_a(0, xx)
-    for i, b in b_order:
+    for k in range(1, Z):
+        zz = _mod(z + k, Z)
+        send(msg.at[zz], r1.at[z], m1_s.at[k - 1], m1_r.at[k - 1], at_z(zz))
+    half = Z // 2
+    for i, b in b_order[0:half]:
         b_second(i, b)
-    chip_b(3)
     for xx in range(X):
         reduce_a(1, xx)
+    chip_b(3)
+    for i, b in b_order[half:]:
+        b_second(i, b)
     reduce_b(0)
 
-    picked = jnp.dot(sel[...], lb[...], preferred_element_type=F32).astype(BF)
-    msg[...] = picked.reshape(Z, g.M, g.T)
-    r1[z] = msg[z]
     for xx in range(X):
         reduce_a(2, xx)
     reduce_b(1)
-    for k in range(1, Z):
-        zz = _mod(z + k, Z)
-        send(msg.at[zz], r1.at[z], m1_s.at[k - 1], m1_r.at[k - 1], at_z(zz))
     for xx in range(X):
         reduce_a(3, xx)
     reduce_b(2)
+    for k in range(1, Z):
+        arrive(r1.at[_mod(z - k, Z)], m1_s.at[k - 1], m1_r.at[k - 1], sibling)
+    m2[...] = jnp.dot(
+        regroup[...], r1[...].reshape(Z * g.M, g.T), preferred_element_type=F32
+    ).astype(BF).reshape(YC, g.M, g.T)
+    r2[yc] = m2[yc]
+    for i, peer, _, _ in yc_peers:
+        send(m2.at[peer], r2.at[yc], m2_s.at[i], m2_r.at[i], at_yc(peer))
+
     for xx in range(X):
         v = own_a(z, xx)
         i = (g.long - 1) * X + xx
@@ -436,14 +450,6 @@
         xx = _mod(x + k, X)
         send(ax_s.at[xx], ax_r.at[k - 1], axx_s.at[k - 1], axx_r.at[k - 1], at_x(xx))
     reduce_b(3)
-    for k in range(1, Z):
-        arrive(r1.at[_mod(z - k, Z)], m1_s.at[k - 1], m1_r.at[k - 1], sibling)
-    m2[...] = jnp.dot(
-        regroup[...], r1[...].reshape(Z * g.M, g.T), preferred_element_type=F32
-    ).astype(BF).reshape(YC, g.M, g.T)
-    r2[yc] = m2[yc]
-    for i, peer, _, _ in yc_peers:
-        send(m2.at[peer], r2.at[yc], m2_s.at[i], m2_r.at[i], at_yc(peer))
 
     va = pa[x, z]
     for k in range(1, X):
@@ -454,8 +460,8 @@
         arrive(bz_r.at[i], bzz_s.at[i], bzz_r.at[i], sibling)
         vb = vb + bz_r[i].astype(F32)
     for k in range(YC):
-        fin_s[k, :, 0:g.a] = va[k * g.t:(k + 1) * g.t]
-        fin_s[k, :, g.a:g.cols] = vb[k * g.t:(k + 1) * g.t]
+        fin_s[k, :, 0:g.ra] = va[k * g.t:(k + 1) * g.t]
+        fin_s[k, :, g.ra:g.cols] = vb[k * g.t:(k + 1) * g.t]
     fin_r[yc] = fin_s[yc]
     for i, peer, _, _ in yc_peers:
         send(fin_s.at[peer], fin_r.at[yc], f_s.at[i], f_r.at[i], at_yc(peer))
@@ -630,12 +636,12 @@
         V((3 * SLOTS * g.dp, 2 * LANES), BF), V((Z * g.M, 3 * SLOTS * g.dp), BF), V((Z * g.M, Z * g.M), BF),
         V((Z * g.M, 2 * LANES), BF),
         V((Z, g.M, g.T), BF), V((Z, g.M, g.T), BF), V((YC, g.M, g.T), BF), V((YC, g.M, g.T), BF),
-        V((X, Z, g.G, g.a), F32), V((X, Z, g.G, g.b), F32),
-        V((g.long, X, g.G, g.a), BF), V((g.long, X, g.G, g.a), BF),
-        V((g.short, X, g.G, g.a), BF), V((g.short, X, g.G, g.a), BF),
-        V((X, g.G, g.a), BF), V((X - 1, g.G, g.a), BF),
-        *[V((Z, g.G, g.b), BF) for _ in range(6)],
-        V((Z - 1, g.G, g.b), BF), V((Z - 1, g.G, g.b), BF),
+        V((X, Z, g.G, g.ra), F32), V((X, Z, g.G, g.rb), F32),
+        V((g.long, X, g.G, g.ra), BF), V((g.long, X, g.G, g.ra), BF),
+        V((g.short, X, g.G, g.ra), BF), V((g.short, X, g.G, g.ra), BF),
+        V((X, g.G, g.ra), BF), V((X - 1, g.G, g.ra), BF),
+        *[V((Z, g.G, g.rb), BF) for _ in range(6)],
+        V((Z - 1, g.G, g.rb), BF), V((Z - 1, g.G, g.rb), BF),
         V((YC, g.t, g.cols), F32), V((YC, g.t, g.cols), F32),
         V((g.wide, g.D), BF), V((g.wide, g.D), BF), V((g.wide, g.D), BF),
         dma((3,)), dma((3,)),

time: 74.5 us -> 71.8 us (0.964)
  Pallas kernels: 73.7 us -> 70.9 us
    pallas_call x1, Pallas kernels: 70.8 us -> 68 us  [per_device(): pl.pallas_call(functools.partial(kernel, g), out_shape=(tok_shape, tok_sh...]
where the time goes in v5:
time: 71.8 us; the launch traced here: 71.6 us
  Pallas kernels  70.9 us (99%)
    pallas_call x1, Pallas kernels, per_device(): pl.pallas_call(functools.partial(kernel, g), out_shape=(tok_shape, tok_sh...  68 us
    pallas_call x1, Pallas kernels, per_device(): pl.pallas_call(functools.partial(hand_over, len(results)), out_shape=tupl...  2.88 us

profile of v5, /device:TPU:1, one launch (start us, length us, event | category | flops | bytes accessed | tf_op | source)
XLA Modules:
  0.0 71.6 jit_solution(4183735368873213820)
XLA Ops:
  0.6 68.0 %widened_layer.1 = (bf16[2,1664]{1,0:T(2,128)(2,1)}, bf16[2,1664]{1,0:T(2,128)(2,1)}, bf16[60,6656]{1,0:T(8,128)(2,1)}, bf16[60,6656]{1,0:T(8,128)(2,1)}, bf16[60,6656]{1,0:T(8,128)(2,1)}) custom-call(bf16[2,1664]{1,0:T(2,128)(2,1)} %refs_0_.1, bf16[2,1664]{1,0:T(2,128)(2,1)} %refs_1_.1, bf16[40,6656]{1,0:T(8,128)(2,1)} %refs_2_.1, ...), custom_call_target="tpu_custom_call" | custom-call | flops 715653120 | bytes 3993600 | tf_op jit(solution)/shard_map/widened_layer/pallas_call | solution.py:660
  68.7 2.9 %hand_over.1 = (bf16[2,1664]{1,0:T(2,128)(2,1)}, bf16[2,1664]{1,0:T(2,128)(2,1)}, bf16[60,6656]{1,0:T(8,128)(2,1)}, bf16[60,6656]{1,0:T(8,128)(2,1)}, bf16[60,6656]{1,0:T(8,128)(2,1)}) custom-call(bf16[2,1664]{1,0:T(2,128)(2,1)} %get-tuple-element.10.refs_0_, bf16[2,1664]{1,0:T(2,128)(2,1)} %get-tuple-element.11.refs_1_, ...), custom_call_target="tpu_custom_call" | custom-call | bytes 4792320 | tf_op jit(solution)/shard_map/hand_over/pallas_call | solution.py:677

commit v6 on v5

--- a/solution.py
+++ b/solution.py
@@ -255,11 +255,11 @@
         b_forward(hop)
         for i, b in slots_at(hop):
             b_across(i, b, last=hop == g.long)
+        for i, b in slots_at(hop - 1):
+            b_pass_on(i, b)
         for j in (0, 1, X - 1, *range(2, X - 1)):
             a_arrive(hop, j)
             a_forward(hop, j)
-        for i, b in slots_at(hop - 1):
-            b_pass_on(i, b)
         for i, b in slots_at(hop):
             a_share(i, b)
         if hop > 1:
@@ -398,6 +398,9 @@
     picked = jnp.dot(sel[...], lb[...], preferred_element_type=F32).astype(BF)
     msg[...] = picked.reshape(Z, g.M, g.T)
     r1[z] = msg[z]
+    for k in range(1, Z):
+        zz = _mod(z + k, Z)
+        send(msg.at[zz], r1.at[z], m1_s.at[k - 1], m1_r.at[k - 1], at_z(zz))
     chip_b(0)
     for i, b in b_order:
         b_first(i, b)
@@ -408,9 +411,6 @@
     for xx in range(X):
         pa[xx] = partial(xx * g.cols, g.ra).reshape(Z, g.G, g.ra)
         reduce_a(0, xx)
-    for k in range(1, Z):
-        zz = _mod(z + k, Z)
-        send(msg.at[zz], r1.at[z], m1_s.at[k - 1], m1_r.at[k - 1], at_z(zz))
     half = Z // 2
     for i, b in b_order[0:half]:
         b_second(i, b)
@@ -590,7 +590,7 @@
     ]
 
 
-PARTS = 4
+PARTS = 2
 
 
 def hand_over(n, *refs):

time: 71.8 us -> 70 us (0.975)
  Pallas kernels: 70.9 us -> 69.2 us
    pallas_call x1, Pallas kernels: 68 us -> 66.5 us  [per_device(): pl.pallas_call(functools.partial(kernel, g), out_shape=(tok_shape, tok_sh...]
where the time goes in v6:
time: 70 us; the launch traced here: 69.8 us
  Pallas kernels  69.2 us (99%)
    pallas_call x1, Pallas kernels, per_device(): pl.pallas_call(functools.partial(kernel, g), out_shape=(tok_shape, tok_sh...  66.5 us
    pallas_call x1, Pallas kernels, per_device(): pl.pallas_call(functools.partial(hand_over, len(results)), out_shape=tupl...  2.68 us

profile of v6, /device:TPU:1, one launch (start us, length us, event | category | flops | bytes accessed | tf_op | source)
XLA Modules:
  0.0 69.8 jit_solution(12751025269967569192)
XLA Ops:
  0.6 66.5 %widened_layer.1 = (bf16[2,1664]{1,0:T(2,128)(2,1)}, bf16[2,1664]{1,0:T(2,128)(2,1)}, bf16[60,6656]{1,0:T(8,128)(2,1)}, bf16[60,6656]{1,0:T(8,128)(2,1)}, bf16[60,6656]{1,0:T(8,128)(2,1)}) custom-call(bf16[2,1664]{1,0:T(2,128)(2,1)} %refs_0_.1, bf16[2,1664]{1,0:T(2,128)(2,1)} %refs_1_.1, bf16[40,6656]{1,0:T(8,128)(2,1)} %refs_2_.1, ...), custom_call_target="tpu_custom_call" | custom-call | flops 715653120 | bytes 3993600 | tf_op jit(solution)/shard_map/widened_layer/pallas_call | solution.py:660
  67.1 2.7 %hand_over.1 = (bf16[2,1664]{1,0:T(2,128)(2,1)}, bf16[2,1664]{1,0:T(2,128)(2,1)}, bf16[60,6656]{1,0:T(8,128)(2,1)}, bf16[60,6656]{1,0:T(8,128)(2,1)}, bf16[60,6656]{1,0:T(8,128)(2,1)}) custom-call(bf16[2,1664]{1,0:T(2,128)(2,1)} %get-tuple-element.10.refs_0_, bf16[2,1664]{1,0:T(2,128)(2,1)} %get-tuple-element.11.refs_1_, ...), custom_call_target="tpu_custom_call" | custom-call | bytes 4792320 | tf_op jit(solution)/shard_map/hand_over/pallas_call | solution.py:677

commit v7 on v6

--- a/solution.py
+++ b/solution.py
@@ -411,12 +411,12 @@
     for xx in range(X):
         pa[xx] = partial(xx * g.cols, g.ra).reshape(Z, g.G, g.ra)
         reduce_a(0, xx)
+    chip_b(3)
     half = Z // 2
     for i, b in b_order[0:half]:
         b_second(i, b)
     for xx in range(X):
         reduce_a(1, xx)
-    chip_b(3)
     for i, b in b_order[half:]:
         b_second(i, b)
     reduce_b(0)

time: 70 us -> 70 us (level)
  no operation moved by 1% of the time
where the time goes in v7:
time: 70 us; the launch traced here: 69.8 us
  Pallas kernels  69.2 us (99%)
    pallas_call x1, Pallas kernels, per_device(): pl.pallas_call(functools.partial(kernel, g), out_shape=(tok_shape, tok_sh...  66.5 us
    pallas_call x1, Pallas kernels, per_device(): pl.pallas_call(functools.partial(hand_over, len(results)), out_shape=tupl...  2.68 us

profile of v7, /device:TPU:1, one launch (start us, length us, event | category | flops | bytes accessed | tf_op | source)
XLA Modules:
  0.0 69.8 jit_solution(7012873532132210827)
XLA Ops:
  0.6 66.5 %widened_layer.1 = (bf16[2,1664]{1,0:T(2,128)(2,1)}, bf16[2,1664]{1,0:T(2,128)(2,1)}, bf16[60,6656]{1,0:T(8,128)(2,1)}, bf16[60,6656]{1,0:T(8,128)(2,1)}, bf16[60,6656]{1,0:T(8,128)(2,1)}) custom-call(bf16[2,1664]{1,0:T(2,128)(2,1)} %refs_0_.1, bf16[2,1664]{1,0:T(2,128)(2,1)} %refs_1_.1, bf16[40,6656]{1,0:T(8,128)(2,1)} %refs_2_.1, ...), custom_call_target="tpu_custom_call" | custom-call | flops 715653120 | bytes 3993600 | tf_op jit(solution)/shard_map/widened_layer/pallas_call | solution.py:660
  67.1 2.7 %hand_over.1 = (bf16[2,1664]{1,0:T(2,128)(2,1)}, bf16[2,1664]{1,0:T(2,128)(2,1)}, bf16[60,6656]{1,0:T(8,128)(2,1)}, bf16[60,6656]{1,0:T(8,128)(2,1)}, bf16[60,6656]{1,0:T(8,128)(2,1)}) custom-call(bf16[2,1664]{1,0:T(2,128)(2,1)} %get-tuple-element.10.refs_0_, bf16[2,1664]{1,0:T(2,128)(2,1)} %get-tuple-element.11.refs_1_, ...), custom_call_target="tpu_custom_call" | custom-call | bytes 4792320 | tf_op jit(solution)/shard_map/hand_over/pallas_call | solution.py:677
